TPU v7x, 512 devices: a whole 4x8x8 slice. The times are simulated.
512 devices in a mesh: frame: 8 (over z_hi, core), patch: 32 (over x, y), tp: 2 (over z_lo).
Axes of the slice: x: 4, y: 8, z: 8 (z_hi: 4, z_lo: 2; z = z_hi * 2 + z_lo), core: 2. Of those that a mesh axis runs over, the one named last changes fastest.
Arguments:
- residual_codes: int32 [16, 64, 32, 1536], P('frame', 'patch', None, 'tp'), may hold values from -127 to 127
- exponents: int32 [16, 64, 32, 24], P('frame', 'patch', None, 'tp'), may hold values from -8 to -4
- conv_weight: bfloat16 [3, 3, 3, 1536], replicated, may hold values from -1.25 to 1.25
- timestep: int32 [16], P('frame'), may hold values from 0 to 49
- modulation: bfloat16 [50, 2, 1536], replicated, may hold values from -3 to 3
- query_weight: bfloat16 [1536, 768], P(None, 'tp')
- key_weight: bfloat16 [1536, 768], P(None, 'tp')
- value_weight: bfloat16 [1536, 768], P(None, 'tp'), may hold values from -0.15625 to 0.15625
Outputs:
- attended: bfloat16 [16, 64, 32, 768], P('frame', 'patch', None, 'tp')
All inputs are finite; a program needn't handle non-finite values.
Results may differ from a plain program's by a relative error of at most 0.02.
The roundings to bfloat16 on the way count: a program that leaves them out, or rounds other values in their place, can miss the bound.
Values may be sent and summed in bfloat16 or wider, within the bound.
No kernel may reach another device: no remote copies, remote signals or barrier semaphores. Data moves between devices by JAX's collectives and lax.ppermute only.
A program may use at most 128 MiB of HBM per device.

v0:
```python
import jax
import jax.numpy as jnp
from jax import lax
from jax.sharding import PartitionSpec as P

HEAD_DIM = 64


def extended(x, sides, width):
    for axis, dim in sides:
        size, length = (lax.axis_size(axis), x.shape[dim])
        up = [(i, (i + 1) % size) for i in range(size - 1)]
        down = [(j, i) for i, j in up]
        last = lax.slice_in_dim(x, length - width, length, axis=dim)
        first = lax.slice_in_dim(x, 0, width, axis=dim)
        before = lax.ppermute(last, axis, up)
        after = lax.ppermute(first, axis, down)
        x = jnp.concatenate([before, x, after], axis=dim)
    return x


def dequantize(residual_codes, exponents):
    groups = exponents.shape[-1]
    channels = residual_codes.shape[-1]
    factor = jnp.exp2(exponents.astype(jnp.float32))
    values = residual_codes.astype(jnp.float32).reshape(
        residual_codes.shape[:-1] + (groups, channels // groups)
    )
    return (values * factor[..., None]).reshape(residual_codes.shape)


def convolve(padded, kernel, out_shape):
    frames, tile_rows, tile_cols = out_shape
    widened = jnp.pad(padded, ((0, 0), (0, 0), (1, 1), (0, 0)))
    result = jnp.zeros(out_shape + (kernel.shape[-1],), jnp.float32)
    for shift_f in range(3):
        for shift_h in range(3):
            for shift_w in range(3):
                window = widened[
                    shift_f : shift_f + frames,
                    shift_h : shift_h + tile_rows,
                    shift_w : shift_w + tile_cols,
                    :,
                ]
                result = result + window.astype(jnp.float32) * kernel[
                    shift_f, shift_h, shift_w
                ].astype(jnp.float32)
    return result


def modulate(mixed, modulation, timestep):
    selector = (
        jnp.arange(modulation.shape[0], dtype=jnp.int32)[None, :] == timestep[:, None]
    ).astype(jnp.float32)
    picked = jnp.einsum("fs,sjd->fjd", selector, modulation.astype(jnp.float32))
    shift_rows = picked[:, 0][:, None, None, :]
    scale_rows = picked[:, 1][:, None, None, :]
    values = mixed.astype(jnp.float32)
    average = jnp.mean(values, axis=-1, keepdims=True)
    centered = values - average
    variance = jnp.mean(centered * centered, axis=-1, keepdims=True)
    normed = centered / jnp.sqrt(variance + 1e-06) * (1.0 + scale_rows) + shift_rows
    return normed.astype(jnp.bfloat16)


def local(
    residual_codes,
    exponents,
    conv_weight,
    timestep,
    modulation,
    query_weight,
    key_weight,
    value_weight,
):
    frames, tile_rows, tile_cols, channels = residual_codes.shape
    model_width = conv_weight.shape[-1]
    local_width = query_weight.shape[1]
    local_heads = local_width // HEAD_DIM
    token_count = frames * tile_rows * tile_cols
    grid_shape = (frames, tile_rows, tile_cols)
    inputs_exact = dequantize(residual_codes, exponents)
    inputs_narrow = inputs_exact.astype(jnp.bfloat16)
    pair_index = lax.axis_index("tp")
    kernel = lax.dynamic_slice_in_dim(conv_weight, pair_index * channels, channels, 3)
    padded = extended(inputs_narrow, (("frame", 0), ("patch", 1)), 1)
    mixed_half = (inputs_exact + convolve(padded, kernel, grid_shape)).astype(jnp.bfloat16)
    mixed = lax.all_gather(mixed_half, "tp", axis=3, tiled=True)
    normed = modulate(mixed, modulation, timestep).reshape(token_count, model_width)
    queries = jnp.dot(normed, query_weight, preferred_element_type=jnp.float32).astype(jnp.bfloat16)
    key_local = jnp.dot(normed, key_weight, preferred_element_type=jnp.float32).astype(jnp.bfloat16)
    value_local = jnp.dot(normed, value_weight, preferred_element_type=jnp.float32).astype(
        jnp.bfloat16
    )
    score_scale = HEAD_DIM ** (-0.5)
    query_heads = queries.reshape(token_count, local_heads, HEAD_DIM)

    def fold_keys(state_tuple, shard_pair):
        running_max, running_sum, weighted = state_tuple
        key_part, value_part = shard_pair
        count_rows = key_part.shape[0]
        key_heads = key_part.reshape(count_rows, local_heads, HEAD_DIM)
        value_heads = value_part.reshape(count_rows, local_heads, HEAD_DIM)
        scores = (
            jnp.einsum("qhd,khd->hqk", query_heads, key_heads, preferred_element_type=jnp.float32)
            * score_scale
        )
        new_max = jnp.maximum(running_max, jnp.max(scores, axis=2))
        rescale = jnp.exp(running_max - new_max)
        exps = jnp.exp(scores - new_max[:, :, None])
        running_sum = running_sum * rescale + jnp.sum(exps, axis=2)
        update = jnp.einsum(
            "hqk,khd->qhd",
            exps.astype(jnp.bfloat16),
            value_heads,
            preferred_element_type=jnp.float32,
        )
        weighted = weighted * jnp.transpose(rescale)[:, :, None] + update
        return (new_max, running_sum, weighted)

    initial = (
        jnp.full((local_heads, token_count), -jnp.inf, jnp.float32),
        jnp.zeros((local_heads, token_count), jnp.float32),
        jnp.zeros((token_count, local_heads, HEAD_DIM), jnp.float32),
    )
    key_all, value_all = (
        lax.all_gather(key_local, "patch", axis=0, tiled=True),
        lax.all_gather(value_local, "patch", axis=0, tiled=True),
    )
    span_rows = 4 * token_count
    block_count = key_all.shape[0] // span_rows
    stacked = (
        key_all.reshape(block_count, span_rows, local_width),
        value_all.reshape(block_count, span_rows, local_width),
    )

    def visit(state_tuple, shard_pair):
        return (fold_keys(state_tuple, shard_pair), None)

    final_state, unused_out = lax.scan(visit, initial, stacked)
    weighted = final_state[2] / jnp.transpose(final_state[1])[:, :, None]
    return weighted.astype(jnp.bfloat16).reshape(frames, tile_rows, tile_cols, local_width)


def solution(mesh):
    in_specs = (
        P("frame", "patch", None, "tp"),
        P("frame", "patch", None, "tp"),
        P(),
        P("frame"),
        P(),
        P(None, "tp"),
        P(None, "tp"),
        P(None, "tp"),
    )
    out_specs = P("frame", "patch", None, "tp")
    return jax.shard_map(local, mesh=mesh, in_specs=in_specs, out_specs=out_specs, check_vma=False)
```

profile of v0, /device:TPU:8, one launch (start us, length us, event | category | flops | bytes accessed | tf_op | source)
XLA Modules:
  0.0 246.6 jit_solution(11231171021607628593)
XLA Ops:
  6.5 0.9 multiply_exponential_fusion
  8.3 1.7 collective-permute-start
  10.0 1.3 collective-permute-start.1
  11.6 5.6 %collective-permute-done.1 = bf16[1,2,32,768]{3,2,1,0:T(8,128)(2,1)S(1)} collective-permute-done((bf16[1,2,32,768]{3,2,1,0:T(8,128)(2,1)S(1)}, bf16[1,2,32,768]{3,2,1,0:T(8,128)(2,1)S(1)}, u32[]{:S(2)}, u32[]{:S(2)}) %collective-permute-start.1) | collective-permute-done | bytes 98336 | tf_op jit(solution)/shard_map/ppermute | solution.py:17
  17.3 3.5 %collective-permute-start.2 = (bf16[4,1,32,768]{3,2,1,0:T(8,128)(2,1)S(1)}, bf16[4,1,32,768]{3,2,1,0:T(8,128)(2,1)S(1)}, u32[]{:S(2)}, u32[]{:S(2)}) collective-permute-start(bf16[4,1,32,768]{3,2,1,0:T(8,128)(2,1)S(1)} %get-tuple-element.132), channel_id=1, source_target_pairs={{0,2},{2,4},{4,6},{6,8},{8,10},{10,12},{12,14},{14,16},{16,18},{18... | collective-permute-start | bytes 589832 | tf_op jit(solution)/shard_map/ppermute | solution.py:16
  20.8 2.4 collective-permute-start.3
  23.5 1.4 collective-permute-done.2
  24.8 3.5 %collective-permute-done.3 = bf16[4,1,32,768]{3,2,1,0:T(8,128)(2,1)S(1)} collective-permute-done((bf16[4,1,32,768]{3,2,1,0:T(8,128)(2,1)S(1)}, bf16[4,1,32,768]{3,2,1,0:T(8,128)(2,1)S(1)}, u32[]{:S(2)}, u32[]{:S(2)}) %collective-permute-start.3) | collective-permute-done | bytes 196640 | tf_op jit(solution)/shard_map/ppermute | solution.py:17
  28.8 1.2 add_convert_fusion
  29.9 6.7 %all_gather.9 = bf16[2,2,32,1536]{3,2,1,0:T(8,128)(2,1)S(1)} all-gather(bf16[2,2,32,768]{3,2,1,0:T(8,128)(2,1)S(1)} %add_convert_fusion), channel_id=1, replica_groups=mesh['frame'=8,'patch'=32,'tp'=2] {'tp'}, dimensions={3}, use_global_device_ids=true | all-gather | bytes 589824 | tf_op jit(solution)/shard_map/all_gather | solution.py:88
  37.3 1.0 convolution_convert_fusion
  38.4 1.0 convolution_convert_fusion.2
  39.5 1.6 convolution_convert_fusion.1
  41.3 90.3 %all-gather.5.cloned.1.call-done = bf16[4096,384]{1,0:T(8,128)(2,1)} async-done(((bf16[128,384]{1,0:T(8,128)(2,1)}), bf16[4096,384]{1,0:T(8,128)(2,1)}) %all-gather.5.cloned.1.call-update) | async-done | bytes 3145744 | tf_op jit(solution)/shard_map/all_gather | solution.py:128
  131.6 85.3 %all-gather.3.cloned.1.call-done = bf16[4096,384]{1,0:T(8,128)(2,1)} async-done(((bf16[128,384]{1,0:T(8,128)(2,1)}), bf16[4096,384]{1,0:T(8,128)(2,1)}) %all-gather.3.cloned.1.call-update) | async-done | bytes 3145744 | tf_op jit(solution)/shard_map/all_gather | solution.py:127
  216.8 21.8 %while.15 = (s32[]{:T(128)}, f32[6,128]{1,0:T(8,128)S(1)}, f32[6,128]{1,0:T(8,128)S(1)}, f32[128,6,64]{0,2,1:T(8,128)S(1)}, bf16[8,512,384]{2,1,0:T(8,128)(2,1)}...) while((s32[]{:T(128)}, f32[6,128]{1,0:T(8,128)S(1)}, ...), condition=%wide.region_5.6_spmd.clone, body=%wide.region_2.5_spmd.clone.sunk | while | flops 103174656 | bytes 9191541 | solution.py:140
  216.8 1.2 constant_dynamic-slice_fusion.22
  218.4 0.4 bitcast_reduce_fusion.2
  219.5 1.2 constant_dynamic-slice_fusion.22
  221.1 0.4 bitcast_reduce_fusion.2
  222.3 1.2 constant_dynamic-slice_fusion.22
  223.9 0.4 bitcast_reduce_fusion.2
  225.0 1.2 constant_dynamic-slice_fusion.22
  226.6 0.4 bitcast_reduce_fusion.2
  227.7 1.2 constant_dynamic-slice_fusion.22
  229.3 0.4 bitcast_reduce_fusion.2
  230.5 1.2 constant_dynamic-slice_fusion.22
  232.1 0.4 bitcast_reduce_fusion.2
  233.2 1.2 constant_dynamic-slice_fusion.22
  235.9 1.2 constant_dynamic-slice_fusion.22
  237.5 0.4 bitcast_reduce_fusion.2
  238.9 0.9 reshape.57
  (97 shorter events, 11.6 us)
Async XLA Ops:
  6.5 30.8 %copy-start = (bf16[1536,384]{1,0:T(8,128)(2,1)S(1)}, bf16[1536,384]{1,0:T(8,128)(2,1)}, u32[]{:S(2)}) copy-start(bf16[1536,384]{1,0:T(8,128)(2,1)} %param.17) | copy-start | bytes 3538948
  6.5 1.6 copy-start.1
  6.5 125.0 %all-gather.5.cloned.1.call-start = ((), (), s32[]{:S(2)}) async-start(), calls=%async_computation.1 | async-start | bytes 3244032 | tf_op jit(solution)/shard_map/all_gather | solution.py:128
  7.9 3.5 %copy-start.3 = (bf16[50,2,1536]{2,1,0:T(2,128)(2,1)S(1)}, bf16[50,2,1536]{2,1,0:T(2,128)(2,1)}, u32[]{:S(2)}) copy-start(bf16[50,2,1536]{2,1,0:T(2,128)(2,1)} %param.14) | copy-start | bytes 921604
  7.9 3.5 %copy-start.5 = (s32[2]{0:T(128)S(1)}, s32[2]{0:T(128)}, u32[]{:S(2)}) copy-start(s32[2]{0:T(128)} %param.13) | copy-start | bytes 28
  8.2 15.0 %copy-start.4 = (bf16[3,3,3,1536]{3,2,1,0:T(4,128)(2,1)S(1)}, bf16[3,3,3,1536]{3,2,1,0:T(4,128)(2,1)}, u32[]{:S(2)}) copy-start(bf16[3,3,3,1536]{3,2,1,0:T(4,128)(2,1)} %param.12) | copy-start | bytes 248836
  8.3 3.3 %collective-permute-start = (bf16[1,2,32,768]{3,2,1,0:T(8,128)(2,1)S(1)}, bf16[1,2,32,768]{3,2,1,0:T(8,128)(2,1)S(1)}, u32[]{:S(2)}, u32[]{:S(2)}) collective-permute-start(bf16[1,2,32,768]{3,2,1,0:T(8,128)(2,1)S(1)} %get-tuple-element.134), channel_id=1, source_target_pairs={{0,64},{64,128},{128,192},{192,256},{256,320},{320,384},{384,448},... | collective-permute-start | bytes 294920 | tf_op jit(solution)/shard_map/ppermute | solution.py:16
  10.0 7.2 %collective-permute-start.1 = (bf16[1,2,32,768]{3,2,1,0:T(8,128)(2,1)S(1)}, bf16[1,2,32,768]{3,2,1,0:T(8,128)(2,1)S(1)}, u32[]{:S(2)}, u32[]{:S(2)}) collective-permute-start(bf16[1,2,32,768]{3,2,1,0:T(8,128)(2,1)S(1)} %get-tuple-element.135), channel_id=1, source_target_pairs={{64,0},{128,64},{192,128},{256,192},{320,256},{384,320},{448,384},... | collective-permute-start | bytes 294920 | tf_op jit(solution)/shard_map/ppermute | solution.py:17
  17.3 7.6 %collective-permute-start.2 = (bf16[4,1,32,768]{3,2,1,0:T(8,128)(2,1)S(1)}, bf16[4,1,32,768]{3,2,1,0:T(8,128)(2,1)S(1)}, u32[]{:S(2)}, u32[]{:S(2)}) collective-permute-start(bf16[4,1,32,768]{3,2,1,0:T(8,128)(2,1)S(1)} %get-tuple-element.132), channel_id=1, source_target_pairs={{0,2},{2,4},{4,6},{6,8},{8,10},{10,12},{12,14},{14,16},{16,18},{18... | collective-permute-start | bytes 589832 | tf_op jit(solution)/shard_map/ppermute | solution.py:16
  20.8 7.6 %collective-permute-start.3 = (bf16[4,1,32,768]{3,2,1,0:T(8,128)(2,1)S(1)}, bf16[4,1,32,768]{3,2,1,0:T(8,128)(2,1)S(1)}, u32[]{:S(2)}, u32[]{:S(2)}) collective-permute-start(bf16[4,1,32,768]{3,2,1,0:T(8,128)(2,1)S(1)} %get-tuple-element.133), channel_id=1, source_target_pairs={{2,0},{4,2},{6,4},{8,6},{10,8},{12,10},{14,12},{16,14},{18,16},{20... | collective-permute-start | bytes 589832 | tf_op jit(solution)/shard_map/ppermute | solution.py:17
  36.8 1.6 copy-start.2
  38.3 178.5 %all-gather.3.cloned.1.call-start = ((), (), s32[]{:S(2)}) async-start(), calls=%async_computation | async-start | bytes 3244032 | tf_op jit(solution)/shard_map/all_gather | solution.py:127
Sparse Core Ops, SparseCore 0:
  38.5 93.0 all-gather.4
  134.7 82.0 all-gather.2
where the time goes:
time: 247 us
  waiting for transfers between devices  186 us (75%)
  local copies, waits for them, and re-layouts  14.6 us (6%)
  between operations  13.6 us (6%)
  matrix products  10.6 us (4%)
  starting transfers between devices  8.93 us (4%)
  blocking collectives  6.71 us (3%)
  other arithmetic  5.49 us (2%)
    all_gather x1, waiting for transfers between devices, local(): lax.all_gather(value_local, 'patch', axis=0, tiled=True)  90.3 us
    all_gather x1, waiting for transfers between devices, local(): lax.all_gather(key_local, 'patch', axis=0, tiled=True)  85.3 us
    dynamic_slice x24, local copies, waits for them, and re-layouts, local(): final_state, unused_out = lax.scan(visit, initial, stacked)  12.6 us
    ppermute x2, waiting for transfers between devices, extended(): after = lax.ppermute(first, axis, down)  9.11 us
    all_gather x1, blocking collectives, local(): mixed = lax.all_gather(mixed_half, 'tp', axis=3, tiled=True)  6.71 us
    ppermute x2, starting transfers between devices, extended(): before = lax.ppermute(last, axis, up)  5.23 us
  transfers between devices with their start and end apart: 6, of which 5 were waited for; matrix products, arithmetic and copies ran while one was open for 1% of the time, Pallas kernels for 0%

commit v1 on v0

v1 whole, which is shorter than its diff:
```python
import functools

import jax
import jax.numpy as jnp
from jax import lax
from jax.experimental import pallas as pl
from jax.experimental.pallas import tpu as pltpu
from jax.sharding import PartitionSpec as P

HEAD_DIM = 64
LANES = 128
ROWS = 4
COLS = 8
LOG2E = 1.4426950408889634
X_GROUPS = [[x * COLS + y for x in range(ROWS)] for y in range(COLS)]
Y_GROUPS = [[x * COLS + y for y in range(COLS)] for x in range(ROWS)]


def extended(x, sides, width):
    for axis, dim in sides:
        size, length = (lax.axis_size(axis), x.shape[dim])
        up = [(i, (i + 1) % size) for i in range(size - 1)]
        down = [(j, i) for i, j in up]
        last = lax.slice_in_dim(x, length - width, length, axis=dim)
        first = lax.slice_in_dim(x, 0, width, axis=dim)
        before = lax.ppermute(last, axis, up)
        after = lax.ppermute(first, axis, down)
        x = jnp.concatenate([before, x, after], axis=dim)
    return x


def dequantize(residual_codes, exponents):
    groups = exponents.shape[-1]
    channels = residual_codes.shape[-1]
    factor = jnp.exp2(exponents.astype(jnp.float32))
    values = residual_codes.astype(jnp.float32).reshape(
        residual_codes.shape[:-1] + (groups, channels // groups)
    )
    return (values * factor[..., None]).reshape(residual_codes.shape)


def convolve(padded, kernel, out_shape):
    frames, tile_rows, tile_cols = out_shape
    widened = jnp.pad(padded, ((0, 0), (0, 0), (1, 1), (0, 0)))
    result = jnp.zeros(out_shape + (kernel.shape[-1],), jnp.float32)
    for shift_f in range(3):
        for shift_h in range(3):
            for shift_w in range(3):
                window = widened[
                    shift_f : shift_f + frames,
                    shift_h : shift_h + tile_rows,
                    shift_w : shift_w + tile_cols,
                    :,
                ]
                result = result + window.astype(jnp.float32) * kernel[
                    shift_f, shift_h, shift_w
                ].astype(jnp.float32)
    return result


def low_lanes(shape):
    return lax.broadcasted_iota(jnp.int32, shape, len(shape) - 1) < HEAD_DIM


def swap(x):
    return pltpu.roll(x, HEAD_DIM, x.ndim - 1)


def project_kernel(mixed_ref, shift_ref, scale_ref, wq_ref, wk_ref, wv_ref, out_ref):
    half = mixed_ref.shape[1] // 2
    parts = []
    for f in range(2):
        rows = pl.ds(f * half, half)
        x = jnp.concatenate([mixed_ref[0, rows, :], mixed_ref[1, rows, :]], axis=1)
        x = x.astype(jnp.float32)
        average = jnp.mean(x, axis=1, keepdims=True)
        centered = x - average
        variance = jnp.mean(centered * centered, axis=1, keepdims=True)
        x = centered * lax.rsqrt(variance + 1e-06)
        x = x * (1.0 + scale_ref[f : f + 1, :]) + shift_ref[f : f + 1, :]
        parts.append(x.astype(jnp.bfloat16))
    normed = jnp.concatenate(parts, axis=0)
    tokens = 2 * half
    low_all, low_half = low_lanes((tokens, LANES)), low_lanes((half, LANES))
    q, k, v = [
        jnp.dot(normed, w[...], preferred_element_type=jnp.float32)
        for w in (wq_ref, wk_ref, wv_ref)
    ]
    heads = wq_ref.shape[1] // HEAD_DIM
    for pair in range(heads // 2):
        lanes = slice(pair * LANES, (pair + 1) * LANES)
        qp, kp, vp = q[:, lanes], k[:, lanes], v[:, lanes]
        first, second = qp[:half], qp[half:]
        even, odd = 2 * pair, 2 * pair + 1
        out_ref[even, :tokens, :] = jnp.where(low_all, kp, swap(vp)).astype(jnp.bfloat16)
        out_ref[odd, :tokens, :] = jnp.where(low_all, swap(kp), vp).astype(jnp.bfloat16)
        out_ref[even, tokens:, :] = jnp.where(low_half, first, swap(second)).astype(jnp.bfloat16)
        out_ref[odd, tokens:, :] = jnp.where(low_half, swap(first), second).astype(jnp.bfloat16)
    for slot in range(heads, out_ref.shape[0]):
        out_ref[slot] = jnp.zeros(out_ref.shape[1:], jnp.bfloat16)


def attend_kernel(q_ref, kv_ref, out_ref):
    kv = kv_ref[...]
    keys = kv.shape[0]
    ones_v = jnp.where(low_lanes((keys, LANES)), jnp.ones_like(kv), kv)
    slots, half, _ = q_ref.shape
    step = 2
    rows = step * half
    low = low_lanes((rows, LANES))
    factor = LOG2E * HEAD_DIM ** (-0.5)
    for i in range(0, slots, step):
        packed = q_ref[i : i + step].reshape(rows, LANES).astype(jnp.float32)
        first = jnp.where(low, packed, 0.0)
        second = jnp.where(low, swap(packed), 0.0)
        queries = jnp.concatenate([first, second], axis=0).astype(jnp.bfloat16)
        scores = lax.dot_general(
            queries, kv, (((1,), (1,)), ((), ())), preferred_element_type=jnp.float32
        )
        top = jnp.max(scores, axis=1, keepdims=True)
        weights = jnp.exp2((scores - top) * factor).astype(jnp.bfloat16)
        summed = jnp.dot(weights, ones_v, preferred_element_type=jnp.float32)
        done = summed / swap(summed)
        result = jnp.where(low, swap(done[:rows]), done[rows:])
        out_ref[i : i + step] = result.astype(jnp.bfloat16).reshape(step, half, LANES)


def unpack_kernel(in_ref, out_ref):
    half = in_ref.shape[1]
    low = low_lanes((half, LANES))
    for pair in range(out_ref.shape[2] // LANES):
        lanes = slice(pair * LANES, (pair + 1) * LANES)
        even = in_ref[2 * pair].astype(jnp.float32)
        odd = in_ref[2 * pair + 1].astype(jnp.float32)
        out_ref[0, :, lanes] = jnp.where(low, even, swap(odd)).astype(jnp.bfloat16)
        out_ref[1, :, lanes] = jnp.where(low, swap(even), odd).astype(jnp.bfloat16)


def call(kernel, shape, *args):
    return pl.pallas_call(
        kernel,
        out_shape=jax.ShapeDtypeStruct(shape, jnp.bfloat16),
        in_specs=[pl.BlockSpec(memory_space=pltpu.VMEM)] * len(args),
        out_specs=pl.BlockSpec(memory_space=pltpu.VMEM),
        compiler_params=pltpu.CompilerParams(vmem_limit_bytes=48 * 1024 * 1024),
    )(*args)


def local(
    residual_codes,
    exponents,
    conv_weight,
    timestep,
    modulation,
    query_weight,
    key_weight,
    value_weight,
):
    frames, tile_rows, tile_cols, channels = residual_codes.shape
    local_width = query_weight.shape[1]
    tokens = frames * tile_rows * tile_cols
    half = tokens // 2
    grid_shape = (frames, tile_rows, tile_cols)
    inputs_exact = dequantize(residual_codes, exponents)
    inputs_narrow = inputs_exact.astype(jnp.bfloat16)
    pair_index = lax.axis_index("tp")
    kernel = lax.dynamic_slice_in_dim(conv_weight, pair_index * channels, channels, 3)
    padded = extended(inputs_narrow, (("frame", 0), ("patch", 1)), 1)
    mixed_half = (inputs_exact + convolve(padded, kernel, grid_shape)).astype(jnp.bfloat16)
    mixed = lax.all_gather(mixed_half.reshape(tokens, channels), "tp", axis=0)
    picked = jnp.take(modulation, timestep, axis=0).astype(jnp.float32)
    send = call(
        project_kernel,
        (COLS, tokens + half, LANES),
        mixed,
        picked[:, 0],
        picked[:, 1],
        query_weight,
        key_weight,
        value_weight,
    )
    held = lax.all_to_all(send, "patch", 0, 0, axis_index_groups=Y_GROUPS)
    kv = lax.all_gather(held[:, :tokens], "patch", axis_index_groups=X_GROUPS, axis=0)
    result = call(
        attend_kernel,
        (COLS, half, LANES),
        held[:, tokens:],
        kv.reshape(ROWS * COLS * tokens, LANES),
    )
    back = lax.all_to_all(result, "patch", 0, 0, axis_index_groups=Y_GROUPS)
    out = call(unpack_kernel, (frames, half, local_width), back)
    return out.reshape(frames, tile_rows, tile_cols, local_width)


def solution(mesh):
    in_specs = (
        P("frame", "patch", None, "tp"),
        P("frame", "patch", None, "tp"),
        P(),
        P("frame"),
        P(),
        P(None, "tp"),
        P(None, "tp"),
        P(None, "tp"),
    )
    out_specs = P("frame", "patch", None, "tp")
    return jax.shard_map(local, mesh=mesh, in_specs=in_specs, out_specs=out_specs, check_vma=False)
```

time: 247 us -> 122 us (0.49)
  the two profiles are of different devices: /device:TPU:8 before, /device:TPU:64 now
where the time goes in v1:
time: 122 us
  blocking collectives  45.4 us (37%)
  waiting for transfers between devices  41.1 us (34%)
  between operations  13.6 us (11%)
  starting transfers between devices  7.95 us (7%)
  Pallas kernels  7.44 us (6%)
  local copies, waits for them, and re-layouts  3.72 us (3%)
  other arithmetic  2.91 us (2%)
    all_gather x1, waiting for transfers between devices, local(): lax.all_gather(held[:, :tokens], 'patch', axis_index_groups=X_GROUPS, axi...  30 us
    all_to_all x1, blocking collectives, local(): held = lax.all_to_all(send, 'patch', 0, 0, axis_index_groups=Y_GROUPS)  23.2 us
    all_to_all x1, blocking collectives, local(): back = lax.all_to_all(result, 'patch', 0, 0, axis_index_groups=Y_GROUPS)  15.6 us
    ppermute x2, waiting for transfers between devices, extended(): after = lax.ppermute(first, axis, down)  9.52 us
    pallas_call x3, Pallas kernels, call(): pl.pallas_call(kernel, out_shape=jax.ShapeDtypeStruct(shape, jnp.bfloat16...  7.44 us
    all_gather x1, blocking collectives, local(): mixed = lax.all_gather(mixed_half.reshape(tokens, channels), 'tp', axis=0)  6.65 us
    ppermute x2, starting transfers between devices, extended(): before = lax.ppermute(last, axis, up)  5.37 us
    ppermute x2, starting transfers between devices, extended(): after = lax.ppermute(first, axis, down)  2.58 us
  transfers between devices with their start and end apart: 5, of which 4 were waited for; matrix products, arithmetic and copies ran while one was open for 1% of the time, Pallas kernels for 0%

profile of v1, /device:TPU:64, one launch (start us, length us, event | category | flops | bytes accessed | tf_op | source)
XLA Modules:
  0.0 122.1 jit_solution(6693501319268776076)
XLA Ops:
  6.5 0.8 multiply_exponential_fusion
  7.3 0.1 copy.12
  7.5 0.3 mul.365
  7.8 0.0 copy-start.7
  7.8 0.3 mul.366
  8.1 0.4 copy-done.5
  8.5 0.0 copy-start.6
  8.5 1.9 %collective-permute-start = (bf16[1,2,32,768]{3,2,1,0:T(8,128)(2,1)S(1)}, bf16[1,2,32,768]{3,2,1,0:T(8,128)(2,1)S(1)}, u32[]{:S(2)}, u32[]{:S(2)}) collective-permute-start(bf16[1,2,32,768]{3,2,1,0:T(8,128)(2,1)S(1)} %get-tuple-element.36), channel_id=1, source_target_pairs={{0,64},{64,128},{128,192},{192,256},{256,320},{320,384},{384,448},... | collective-permute-start | bytes 294920 | tf_op jit(solution)/shard_map/ppermute | solution.py:26
  10.4 1.3 %collective-permute-start.1 = (bf16[1,2,32,768]{3,2,1,0:T(8,128)(2,1)S(1)}, bf16[1,2,32,768]{3,2,1,0:T(8,128)(2,1)S(1)}, u32[]{:S(2)}, u32[]{:S(2)}) collective-permute-start(bf16[1,2,32,768]{3,2,1,0:T(8,128)(2,1)S(1)} %get-tuple-element.37), channel_id=1, source_target_pairs={{64,0},{128,64},{192,128},{256,192},{320,256},{384,320},{448,384},... | collective-permute-start | bytes 294920 | tf_op jit(solution)/shard_map/ppermute | solution.py:27
  11.8 0.6 gather_fusion
  12.4 0.1 fusion.7
  12.5 5.1 %collective-permute-done.1 = bf16[1,2,32,768]{3,2,1,0:T(8,128)(2,1)S(1)} collective-permute-done((bf16[1,2,32,768]{3,2,1,0:T(8,128)(2,1)S(1)}, bf16[1,2,32,768]{3,2,1,0:T(8,128)(2,1)S(1)}, u32[]{:S(2)}, u32[]{:S(2)}) %collective-permute-start.1) | collective-permute-done | bytes 98336 | tf_op jit(solution)/shard_map/ppermute | solution.py:27
  17.7 3.5 %collective-permute-start.2 = (bf16[4,1,32,768]{3,2,1,0:T(8,128)(2,1)S(1)}, bf16[4,1,32,768]{3,2,1,0:T(8,128)(2,1)S(1)}, u32[]{:S(2)}, u32[]{:S(2)}) collective-permute-start(bf16[4,1,32,768]{3,2,1,0:T(8,128)(2,1)S(1)} %get-tuple-element.34), channel_id=1, source_target_pairs={{0,2},{2,4},{4,6},{6,8},{8,10},{10,12},{12,14},{14,16},{16,18},{18... | collective-permute-start | bytes 589832 | tf_op jit(solution)/shard_map/ppermute | solution.py:26
  21.2 1.3 %collective-permute-start.3 = (bf16[4,1,32,768]{3,2,1,0:T(8,128)(2,1)S(1)}, bf16[4,1,32,768]{3,2,1,0:T(8,128)(2,1)S(1)}, u32[]{:S(2)}, u32[]{:S(2)}) collective-permute-start(bf16[4,1,32,768]{3,2,1,0:T(8,128)(2,1)S(1)} %get-tuple-element.35), channel_id=1, source_target_pairs={{2,0},{4,2},{6,4},{8,6},{10,8},{12,10},{14,12},{16,14},{18,16},{20... | collective-permute-start | bytes 589832 | tf_op jit(solution)/shard_map/ppermute | solution.py:27
  22.5 0.3 fusion.11
  22.8 1.5 %collective-permute-done.2 = bf16[4,1,32,768]{3,2,1,0:T(8,128)(2,1)S(1)} collective-permute-done((bf16[4,1,32,768]{3,2,1,0:T(8,128)(2,1)S(1)}, bf16[4,1,32,768]{3,2,1,0:T(8,128)(2,1)S(1)}, u32[]{:S(2)}, u32[]{:S(2)}) %collective-permute-start.2) | collective-permute-done | bytes 196640 | tf_op jit(solution)/shard_map/ppermute | solution.py:26
  24.3 4.4 %collective-permute-done.3 = bf16[4,1,32,768]{3,2,1,0:T(8,128)(2,1)S(1)} collective-permute-done((bf16[4,1,32,768]{3,2,1,0:T(8,128)(2,1)S(1)}, bf16[4,1,32,768]{3,2,1,0:T(8,128)(2,1)S(1)}, u32[]{:S(2)}, u32[]{:S(2)}) %collective-permute-start.3) | collective-permute-done | bytes 196640 | tf_op jit(solution)/shard_map/ppermute | solution.py:27
  28.7 0.1 maximum_maximum_fusion
  28.8 0.3 select_maximum_fusion
  29.2 0.0 copy-start.1
  29.2 0.0 copy-start.2
  29.2 1.2 add_convert_fusion
  30.4 6.6 %all_gather.9.mixed_ref = bf16[2,128,768]{2,1,0:T(8,128)(2,1)S(1)} all-gather(bf16[1,128,768]{2,1,0:T(8,128)(2,1)S(1)} %bitcast.8), channel_id=1, replica_groups=mesh['frame'=8,'patch'=32,'tp'=2] {'tp'}, dimensions={0}, use_global_device_ids=true | all-gather | bytes 589824 | tf_op jit(solution)/shard_map/all_gather | solution.py:170
  37.0 1.2 shard_map.82
  38.2 23.2 %all_to_all.10 = bf16[8,192,128]{2,1,0:T(8,128)(2,1)S(1)} all-to-all(bf16[8,192,128]{2,1,0:T(8,128)(2,1)S(1)} %shard_map.82), channel_id=1, replica_groups={{0,2,4,6,8,10,12,14},{16,18,20,22,24,26,28,30},{32,34,36,38,40,42,44,46..., dimensions={0} | all-to-all | bytes 786432 | tf_op jit(solution)/shard_map/all_to_all | solution.py:182
  61.4 0.7 slice.298
  62.1 0.0 all-gather.3.cloned.1.call-update
  62.1 30.0 %all-gather.3.cloned.1.call-done = bf16[32,128,128]{2,1,0:T(8,128)(2,1)} async-done(((bf16[8,128,128]{2,1,0:T(8,128)(2,1)}), bf16[32,128,128]{2,1,0:T(8,128)(2,1)}) %all-gather.3.cloned.1.call-update) | async-done | bytes 1048592 | tf_op jit(solution)/shard_map/all_gather | solution.py:183
  92.1 1.2 %copy-done.4 = bf16[32,128,128]{2,1,0:T(8,128)(2,1)S(1)} copy-done((bf16[32,128,128]{2,1,0:T(8,128)(2,1)S(1)}, bf16[32,128,128]{2,1,0:T(8,128)(2,1)}, u32[]{:S(2)}) %copy-start.4) | copy-done | bytes 1048600
  93.4 5.5 %shard_map.83 = bf16[8,64,128]{2,1,0:T(8,128)(2,1)S(1)} custom-call(bf16[8,64,128]{2,1,0:T(8,128)(2,1)S(1)} %slice.297.q_ref, bf16[4096,128]{1,0:T(8,128)(2,1)S(1)} %bitcast.7), custom_call_target="tpu_custom_call" | custom-call | tf_op jit(solution)/shard_map/pallas_call | solution.py:140
  98.9 15.6 %all_to_all.11.in_ref = bf16[8,64,128]{2,1,0:T(8,128)(2,1)S(1)} all-to-all(bf16[8,64,128]{2,1,0:T(8,128)(2,1)S(1)} %shard_map.83), channel_id=1, replica_groups={{0,2,4,6,8,10,12,14},{16,18,20,22,24,26,28,30},{32,34,36,38,40,42,44,46..., dimensions={0} | all-to-all | bytes 262144 | tf_op jit(solution)/shard_map/all_to_all | solution.py:190
  114.5 0.7 shard_map.84
  (21 shorter events, 0.2 us)
Async XLA Ops:
  6.5 5.2 %copy-start = (bf16[50,2,1536]{2,1,0:T(2,128)(2,1)S(1)}, bf16[50,2,1536]{2,1,0:T(2,128)(2,1)}, u32[]{:S(2)}) copy-start(bf16[50,2,1536]{2,1,0:T(2,128)(2,1)} %param.12) | copy-start | bytes 921604
  6.5 85.6 %all-gather.3.cloned.1.call-start = ((), (), s32[]{:S(2)}) async-start(), calls=%async_computation.2 | async-start | bytes 1310720 | tf_op jit(solution)/shard_map/all_gather | solution.py:183
  7.5 1.0 copy-start.5
  7.8 3.9 %copy-start.7 = (s32[2]{0:T(128)S(1)}, s32[2]{0:T(128)}, u32[]{:S(2)}) copy-start(s32[2]{0:T(128)} %param.11) | copy-start | bytes 28
  8.5 14.0 %copy-start.6 = (bf16[3,3,3,1536]{3,2,1,0:T(4,128)(2,1)S(1)}, bf16[3,3,3,1536]{3,2,1,0:T(4,128)(2,1)}, u32[]{:S(2)}) copy-start(bf16[3,3,3,1536]{3,2,1,0:T(4,128)(2,1)} %param.10) | copy-start | bytes 248836
  8.5 3.9 %collective-permute-start = (bf16[1,2,32,768]{3,2,1,0:T(8,128)(2,1)S(1)}, bf16[1,2,32,768]{3,2,1,0:T(8,128)(2,1)S(1)}, u32[]{:S(2)}, u32[]{:S(2)}) collective-permute-start(bf16[1,2,32,768]{3,2,1,0:T(8,128)(2,1)S(1)} %get-tuple-element.36), channel_id=1, source_target_pairs={{0,64},{64,128},{128,192},{192,256},{256,320},{320,384},{384,448},... | collective-permute-start | bytes 294920 | tf_op jit(solution)/shard_map/ppermute | solution.py:26
  10.4 7.2 %collective-permute-start.1 = (bf16[1,2,32,768]{3,2,1,0:T(8,128)(2,1)S(1)}, bf16[1,2,32,768]{3,2,1,0:T(8,128)(2,1)S(1)}, u32[]{:S(2)}, u32[]{:S(2)}) collective-permute-start(bf16[1,2,32,768]{3,2,1,0:T(8,128)(2,1)S(1)} %get-tuple-element.37), channel_id=1, source_target_pairs={{64,0},{128,64},{192,128},{256,192},{320,256},{384,320},{448,384},... | collective-permute-start | bytes 294920 | tf_op jit(solution)/shard_map/ppermute | solution.py:27
  17.7 6.7 %collective-permute-start.2 = (bf16[4,1,32,768]{3,2,1,0:T(8,128)(2,1)S(1)}, bf16[4,1,32,768]{3,2,1,0:T(8,128)(2,1)S(1)}, u32[]{:S(2)}, u32[]{:S(2)}) collective-permute-start(bf16[4,1,32,768]{3,2,1,0:T(8,128)(2,1)S(1)} %get-tuple-element.34), channel_id=1, source_target_pairs={{0,2},{2,4},{4,6},{6,8},{8,10},{10,12},{12,14},{14,16},{16,18},{18... | collective-permute-start | bytes 589832 | tf_op jit(solution)/shard_map/ppermute | solution.py:26
  21.2 7.6 %collective-permute-start.3 = (bf16[4,1,32,768]{3,2,1,0:T(8,128)(2,1)S(1)}, bf16[4,1,32,768]{3,2,1,0:T(8,128)(2,1)S(1)}, u32[]{:S(2)}, u32[]{:S(2)}) collective-permute-start(bf16[4,1,32,768]{3,2,1,0:T(8,128)(2,1)S(1)} %get-tuple-element.35), channel_id=1, source_target_pairs={{2,0},{4,2},{6,4},{8,6},{10,8},{12,10},{14,12},{16,14},{18,16},{20... | collective-permute-start | bytes 589832 | tf_op jit(solution)/shard_map/ppermute | solution.py:27
  29.2 7.9 %copy-start.1 = (bf16[1536,384]{1,0:T(8,128)(2,1)S(1)}, bf16[1536,384]{1,0:T(8,128)(2,1)}, u32[]{:S(2)}) copy-start(bf16[1536,384]{1,0:T(8,128)(2,1)} %wq_ref.1) | copy-start | bytes 3538948
  29.2 7.9 %copy-start.2 = (bf16[1536,384]{1,0:T(8,128)(2,1)S(1)}, bf16[1536,384]{1,0:T(8,128)(2,1)}, u32[]{:S(2)}) copy-start(bf16[1536,384]{1,0:T(8,128)(2,1)} %wk_ref.1) | copy-start | bytes 3538948
  29.2 7.9 %copy-start.3 = (bf16[1536,384]{1,0:T(8,128)(2,1)S(1)}, bf16[1536,384]{1,0:T(8,128)(2,1)}, u32[]{:S(2)}) copy-start(bf16[1536,384]{1,0:T(8,128)(2,1)} %wv_ref.1) | copy-start | bytes 3538948
  92.1 1.2 %copy-start.4 = (bf16[32,128,128]{2,1,0:T(8,128)(2,1)S(1)}, bf16[32,128,128]{2,1,0:T(8,128)(2,1)}, u32[]{:S(2)}) copy-start(bf16[32,128,128]{2,1,0:T(8,128)(2,1)} %all-gather.3.cloned.1.call-done) | copy-start | bytes 3145732
Sparse Core Ops, SparseCore 0:
  62.2 29.8 all-gather.2

commit v2 on v1

--- a/solution.py
+++ b/solution.py
@@ -180,7 +180,8 @@
         value_weight,
     )
     held = lax.all_to_all(send, "patch", 0, 0, axis_index_groups=Y_GROUPS)
-    kv = lax.all_gather(held[:, :tokens], "patch", axis_index_groups=X_GROUPS, axis=0)
+    copies = jnp.broadcast_to(held[None, :, :tokens], (ROWS, COLS, tokens, LANES))
+    kv = lax.all_to_all(copies, "patch", 0, 0, axis_index_groups=X_GROUPS)
     result = call(
         attend_kernel,
         (COLS, half, LANES),

time: 122 us -> 94.3 us (0.77)
  the two profiles are of different devices: /device:TPU:64 before, /device:TPU:128 now
where the time goes in v2:
time: 94.3 us; the launch traced here: 94 us
  blocking collectives  39.7 us (42%)
  waiting for transfers between devices  24.9 us (26%)
  starting transfers between devices  15.7 us (17%)
  Pallas kernels  7.48 us (8%)
  local copies, waits for them, and re-layouts  3.01 us (3%)
  other arithmetic  2.91 us (3%)
    all_to_all x1, blocking collectives, local(): held = lax.all_to_all(send, 'patch', 0, 0, axis_index_groups=Y_GROUPS)  21.3 us
    all_to_all x1, waiting for transfers between devices, local(): kv = lax.all_to_all(copies, 'patch', 0, 0, axis_index_groups=X_GROUPS)  16.1 us
    all_to_all x1, blocking collectives, local(): back = lax.all_to_all(result, 'patch', 0, 0, axis_index_groups=Y_GROUPS)  12.1 us
    pallas_call x3, Pallas kernels, call(): pl.pallas_call(kernel, out_shape=jax.ShapeDtypeStruct(shape, jnp.bfloat16...  7.48 us
    ppermute x2, waiting for transfers between devices, extended(): after = lax.ppermute(first, axis, down)  7.3 us
    all_gather x1, blocking collectives, local(): mixed = lax.all_gather(mixed_half.reshape(tokens, channels), 'tp', axis=0)  6.35 us
    ppermute x2, starting transfers between devices, extended(): after = lax.ppermute(first, axis, down)  5.83 us
    ppermute x2, starting transfers between devices, extended(): before = lax.ppermute(last, axis, up)  5.54 us
  transfers between devices with their start and end apart: 5, of which 4 were waited for; matrix products, arithmetic and copies ran while one was open for 1% of the time, Pallas kernels for 0%

profile of v2, /device:TPU:128, one launch (start us, length us, event | category | flops | bytes accessed | tf_op | source)
XLA Modules:
  0.0 94.0 jit_solution(4130584456645240456)
XLA Ops:
  0.0 0.8 multiply_exponential_fusion
  0.8 0.1 copy.12
  0.9 0.3 mul.365
  1.3 0.0 copy-start.6
  1.3 0.3 mul.366
  1.6 0.4 copy-done.4
  2.0 0.0 copy-start.5
  2.0 2.1 %collective-permute-start = (bf16[1,2,32,768]{3,2,1,0:T(8,128)(2,1)S(1)}, bf16[1,2,32,768]{3,2,1,0:T(8,128)(2,1)S(1)}, u32[]{:S(2)}, u32[]{:S(2)}) collective-permute-start(bf16[1,2,32,768]{3,2,1,0:T(8,128)(2,1)S(1)} %get-tuple-element.36), channel_id=1, source_target_pairs={{0,64},{64,128},{128,192},{192,256},{256,320},{320,384},{384,448},... | collective-permute-start | bytes 294920 | tf_op jit(solution)/shard_map/ppermute | solution.py:26
  4.1 4.5 %collective-permute-start.1 = (bf16[1,2,32,768]{3,2,1,0:T(8,128)(2,1)S(1)}, bf16[1,2,32,768]{3,2,1,0:T(8,128)(2,1)S(1)}, u32[]{:S(2)}, u32[]{:S(2)}) collective-permute-start(bf16[1,2,32,768]{3,2,1,0:T(8,128)(2,1)S(1)} %get-tuple-element.37), channel_id=1, source_target_pairs={{64,0},{128,64},{192,128},{256,192},{320,256},{384,320},{448,384},... | collective-permute-start | bytes 294920 | tf_op jit(solution)/shard_map/ppermute | solution.py:27
  8.7 0.6 gather_fusion
  9.2 0.1 fusion.7
  9.3 2.9 %collective-permute-done.1 = bf16[1,2,32,768]{3,2,1,0:T(8,128)(2,1)S(1)} collective-permute-done((bf16[1,2,32,768]{3,2,1,0:T(8,128)(2,1)S(1)}, bf16[1,2,32,768]{3,2,1,0:T(8,128)(2,1)S(1)}, u32[]{:S(2)}, u32[]{:S(2)}) %collective-permute-start.1) | collective-permute-done | bytes 98336 | tf_op jit(solution)/shard_map/ppermute | solution.py:27
  12.3 3.5 %collective-permute-start.2 = (bf16[4,1,32,768]{3,2,1,0:T(8,128)(2,1)S(1)}, bf16[4,1,32,768]{3,2,1,0:T(8,128)(2,1)S(1)}, u32[]{:S(2)}, u32[]{:S(2)}) collective-permute-start(bf16[4,1,32,768]{3,2,1,0:T(8,128)(2,1)S(1)} %get-tuple-element.34), channel_id=1, source_target_pairs={{0,2},{2,4},{4,6},{6,8},{8,10},{10,12},{12,14},{14,16},{16,18},{18... | collective-permute-start | bytes 589832 | tf_op jit(solution)/shard_map/ppermute | solution.py:26
  15.8 1.3 %collective-permute-start.3 = (bf16[4,1,32,768]{3,2,1,0:T(8,128)(2,1)S(1)}, bf16[4,1,32,768]{3,2,1,0:T(8,128)(2,1)S(1)}, u32[]{:S(2)}, u32[]{:S(2)}) collective-permute-start(bf16[4,1,32,768]{3,2,1,0:T(8,128)(2,1)S(1)} %get-tuple-element.35), channel_id=1, source_target_pairs={{2,0},{4,2},{6,4},{8,6},{10,8},{12,10},{14,12},{16,14},{18,16},{20... | collective-permute-start | bytes 589832 | tf_op jit(solution)/shard_map/ppermute | solution.py:27
  17.2 0.3 fusion.11
  17.5 1.5 %collective-permute-done.2 = bf16[4,1,32,768]{3,2,1,0:T(8,128)(2,1)S(1)} collective-permute-done((bf16[4,1,32,768]{3,2,1,0:T(8,128)(2,1)S(1)}, bf16[4,1,32,768]{3,2,1,0:T(8,128)(2,1)S(1)}, u32[]{:S(2)}, u32[]{:S(2)}) %collective-permute-start.2) | collective-permute-done | bytes 196640 | tf_op jit(solution)/shard_map/ppermute | solution.py:26
  19.0 4.4 %collective-permute-done.3 = bf16[4,1,32,768]{3,2,1,0:T(8,128)(2,1)S(1)} collective-permute-done((bf16[4,1,32,768]{3,2,1,0:T(8,128)(2,1)S(1)}, bf16[4,1,32,768]{3,2,1,0:T(8,128)(2,1)S(1)}, u32[]{:S(2)}, u32[]{:S(2)}) %collective-permute-start.3) | collective-permute-done | bytes 196640 | tf_op jit(solution)/shard_map/ppermute | solution.py:27
  23.4 0.1 maximum_maximum_fusion
  23.5 0.3 select_maximum_fusion
  23.8 0.0 copy-start.1
  23.9 0.0 copy-start.2
  23.9 0.0 copy-start.3
  23.9 1.2 %add_convert_fusion = bf16[2,2,32,768]{3,2,1,0:T(8,128)(2,1)S(1)} fusion(bf16[2,2,32,768]{3,2,1,0:T(8,128)(2,1)S(1)} %fusion.6, bf16[4,4,34,768]{3,2,1,0:T(8,128)(2,1)S(1)} %select_maximum_fusion, bf16[4,3,32,768]{3,2,1,0:T(8,128)(2,1)S(1)} %get-tuple-element.33, bf16[1,2,32,768]{3,2,1,0:T(8,128)(2,1)S(1)} %collective-permute-done.1, ...), kind=kLoop, calls=%fused_computation.14 | loop fusion | flops 8454144 | bytes 6177792 | tf_op jit(solution)/shard_map/convert_element_type | solution.py:169
  25.1 6.3 %all_gather.3.mixed_ref = bf16[2,128,768]{2,1,0:T(8,128)(2,1)S(1)} all-gather(bf16[1,128,768]{2,1,0:T(8,128)(2,1)S(1)} %bitcast.8), channel_id=1, replica_groups=mesh['frame'=8,'patch'=32,'tp'=2] {'tp'}, dimensions={0}, use_global_device_ids=true | all-gather | bytes 589824 | tf_op jit(solution)/shard_map/all_gather | solution.py:170
  31.4 1.2 %shard_map.82 = bf16[8,192,128]{2,1,0:T(8,128)(2,1)S(1)} custom-call(bf16[2,128,768]{2,1,0:T(8,128)(2,1)S(1)} %all_gather.3.mixed_ref, f32[2,1536]{1,0:T(2,128)S(1)} %get-tuple-element.39.shift_ref, f32[2,1536]{1,0:T(2,128)S(1)} %get-tuple-element.38.scale_ref, bf16[1536,384]{1,0:T(8,128)(2,1)S(1)} %copy-done.1, bf16[1536,384]{1,0:T(8,128)(2,1)S(1)} %copy-done.2, ...), custom_call_target="tpu_custom_call" | custom-call | tf_op jit(solution)/shard_map/pallas_call | solution.py:140
  32.6 21.3 %all_to_all.15 = bf16[8,192,128]{2,1,0:T(8,128)(2,1)S(1)} all-to-all(bf16[8,192,128]{2,1,0:T(8,128)(2,1)S(1)} %shard_map.82), channel_id=1, replica_groups={{0,2,4,6,8,10,12,14},{16,18,20,22,24,26,28,30},{32,34,36,38,40,42,44,46..., dimensions={0} | all-to-all | bytes 786432 | tf_op jit(solution)/shard_map/all_to_all | solution.py:182
  53.9 1.2 %broadcast_in_dim.14 = bf16[4,8,128,128]{3,2,1,0:T(8,128)(2,1)} broadcast(bf16[8,128,128]{2,1,0:T(8,128)(2,1)S(1)} %slice.298), dimensions={1,2,3} | broadcast | bytes 1310720 | tf_op jit(solution)/shard_map/broadcast_in_dim | solution.py:183
  55.1 4.3 %all-to-all-start.1 = ((bf16[4,8,128,128]{3,2,1,0:T(8,128)(2,1)}), bf16[4,8,128,128]{3,2,1,0:T(8,128)(2,1)S(1)}, u32[]{:S(2)}, u32[]{:S(2)}) async-start(bf16[4,8,128,128]{3,2,1,0:T(8,128)(2,1)} %broadcast_in_dim.14), calls=%async_computation.1 | async-start | bytes 2097152 | tf_op jit(solution)/shard_map/all_to_all | solution.py:184
  59.4 16.1 %all-to-all-done.1 = bf16[4,8,128,128]{3,2,1,0:T(8,128)(2,1)S(1)} async-done(((bf16[4,8,128,128]{3,2,1,0:T(8,128)(2,1)}), bf16[4,8,128,128]{3,2,1,0:T(8,128)(2,1)S(1)}, u32[]{:S(2)}, u32[]{:S(2)}) %all-to-all-start.1) | async-done | bytes 1048608 | tf_op jit(solution)/shard_map/all_to_all | solution.py:184
  75.5 5.6 %shard_map.83 = bf16[8,64,128]{2,1,0:T(8,128)(2,1)S(1)} custom-call(bf16[8,64,128]{2,1,0:T(8,128)(2,1)S(1)} %slice.297.q_ref, bf16[4096,128]{1,0:T(8,128)(2,1)S(1)} %bitcast.7), custom_call_target="tpu_custom_call" | custom-call | tf_op jit(solution)/shard_map/pallas_call | solution.py:140
  81.1 12.1 %all_to_all.16.in_ref = bf16[8,64,128]{2,1,0:T(8,128)(2,1)S(1)} all-to-all(bf16[8,64,128]{2,1,0:T(8,128)(2,1)S(1)} %shard_map.83), channel_id=1, replica_groups={{0,2,4,6,8,10,12,14},{16,18,20,22,24,26,28,30},{32,34,36,38,40,42,44,46..., dimensions={0} | all-to-all | bytes 262144 | tf_op jit(solution)/shard_map/all_to_all | solution.py:191
  93.2 0.7 shard_map.84
  (19 shorter events, 0.2 us)
Async XLA Ops:
  0.0 8.7 %copy-start = (bf16[50,2,1536]{2,1,0:T(2,128)(2,1)S(1)}, bf16[50,2,1536]{2,1,0:T(2,128)(2,1)}, u32[]{:S(2)}) copy-start(bf16[50,2,1536]{2,1,0:T(2,128)(2,1)} %param.12) | copy-start | bytes 921604
  0.9 1.0 %copy-start.4 = (s32[2,2,32,768]{3,2,1,0:T(8,128)S(1)}, s32[2,2,32,768]{3,2,1,0:T(8,128)}, u32[]{:S(2)}) copy-start(s32[2,2,32,768]{3,2,1,0:T(8,128)} %param.8) | copy-start | bytes 1179652
  1.3 7.3 %copy-start.6 = (s32[2]{0:T(128)S(1)}, s32[2]{0:T(128)}, u32[]{:S(2)}) copy-start(s32[2]{0:T(128)} %param.11) | copy-start | bytes 28
  2.0 15.2 %copy-start.5 = (bf16[3,3,3,1536]{3,2,1,0:T(4,128)(2,1)S(1)}, bf16[3,3,3,1536]{3,2,1,0:T(4,128)(2,1)}, u32[]{:S(2)}) copy-start(bf16[3,3,3,1536]{3,2,1,0:T(4,128)(2,1)} %param.10) | copy-start | bytes 248836
  2.0 7.3 %collective-permute-start = (bf16[1,2,32,768]{3,2,1,0:T(8,128)(2,1)S(1)}, bf16[1,2,32,768]{3,2,1,0:T(8,128)(2,1)S(1)}, u32[]{:S(2)}, u32[]{:S(2)}) collective-permute-start(bf16[1,2,32,768]{3,2,1,0:T(8,128)(2,1)S(1)} %get-tuple-element.36), channel_id=1, source_target_pairs={{0,64},{64,128},{128,192},{192,256},{256,320},{320,384},{384,448},... | collective-permute-start | bytes 294920 | tf_op jit(solution)/shard_map/ppermute | solution.py:26
  4.1 8.2 %collective-permute-start.1 = (bf16[1,2,32,768]{3,2,1,0:T(8,128)(2,1)S(1)}, bf16[1,2,32,768]{3,2,1,0:T(8,128)(2,1)S(1)}, u32[]{:S(2)}, u32[]{:S(2)}) collective-permute-start(bf16[1,2,32,768]{3,2,1,0:T(8,128)(2,1)S(1)} %get-tuple-element.37), channel_id=1, source_target_pairs={{64,0},{128,64},{192,128},{256,192},{320,256},{384,320},{448,384},... | collective-permute-start | bytes 294920 | tf_op jit(solution)/shard_map/ppermute | solution.py:27
  12.3 6.7 %collective-permute-start.2 = (bf16[4,1,32,768]{3,2,1,0:T(8,128)(2,1)S(1)}, bf16[4,1,32,768]{3,2,1,0:T(8,128)(2,1)S(1)}, u32[]{:S(2)}, u32[]{:S(2)}) collective-permute-start(bf16[4,1,32,768]{3,2,1,0:T(8,128)(2,1)S(1)} %get-tuple-element.34), channel_id=1, source_target_pairs={{0,2},{2,4},{4,6},{6,8},{8,10},{10,12},{12,14},{14,16},{16,18},{18... | collective-permute-start | bytes 589832 | tf_op jit(solution)/shard_map/ppermute | solution.py:26
  15.8 7.6 %collective-permute-start.3 = (bf16[4,1,32,768]{3,2,1,0:T(8,128)(2,1)S(1)}, bf16[4,1,32,768]{3,2,1,0:T(8,128)(2,1)S(1)}, u32[]{:S(2)}, u32[]{:S(2)}) collective-permute-start(bf16[4,1,32,768]{3,2,1,0:T(8,128)(2,1)S(1)} %get-tuple-element.35), channel_id=1, source_target_pairs={{2,0},{4,2},{6,4},{8,6},{10,8},{12,10},{14,12},{16,14},{18,16},{20... | collective-permute-start | bytes 589832 | tf_op jit(solution)/shard_map/ppermute | solution.py:27
  23.8 7.6 %copy-start.1 = (bf16[1536,384]{1,0:T(8,128)(2,1)S(1)}, bf16[1536,384]{1,0:T(8,128)(2,1)}, u32[]{:S(2)}) copy-start(bf16[1536,384]{1,0:T(8,128)(2,1)} %wq_ref.1) | copy-start | bytes 3538948
  23.9 7.6 %copy-start.2 = (bf16[1536,384]{1,0:T(8,128)(2,1)S(1)}, bf16[1536,384]{1,0:T(8,128)(2,1)}, u32[]{:S(2)}) copy-start(bf16[1536,384]{1,0:T(8,128)(2,1)} %wk_ref.1) | copy-start | bytes 3538948
  23.9 7.6 %copy-start.3 = (bf16[1536,384]{1,0:T(8,128)(2,1)S(1)}, bf16[1536,384]{1,0:T(8,128)(2,1)}, u32[]{:S(2)}) copy-start(bf16[1536,384]{1,0:T(8,128)(2,1)} %wv_ref.1) | copy-start | bytes 3538948
  55.1 20.4 %all-to-all-start.1 = ((bf16[4,8,128,128]{3,2,1,0:T(8,128)(2,1)}), bf16[4,8,128,128]{3,2,1,0:T(8,128)(2,1)S(1)}, u32[]{:S(2)}, u32[]{:S(2)}) async-start(bf16[4,8,128,128]{3,2,1,0:T(8,128)(2,1)} %broadcast_in_dim.14), calls=%async_computation.1 | async-start | bytes 2097152 | tf_op jit(solution)/shard_map/all_to_all | solution.py:184

commit v3 on v2

v3 whole, which is shorter than its diff:
```python
import jax
import jax.numpy as jnp
from jax import lax
from jax.experimental import pallas as pl
from jax.experimental.pallas import tpu as pltpu
from jax.sharding import PartitionSpec as P

HEAD_DIM = 64
LANES = 128
ROWS = 4
COLS = 8
LOG2E = 1.4426950408889634
X_GROUPS = [[x * COLS + y for x in range(ROWS)] for y in range(COLS)]
Y_GROUPS = [[x * COLS + y for y in range(COLS)] for x in range(ROWS)]


BLOCK = 64
LEAST = 16


def dequantize_kernel(codes_ref, exponents_ref, *out_refs):
    frames, rows, cols, channels = codes_ref.shape
    groups = exponents_ref.shape[-1]
    tokens = rows * cols
    group = lax.broadcasted_iota(jnp.int32, (groups, channels), 0)
    owner = lax.broadcasted_iota(jnp.int32, (groups, channels), 1) // BLOCK
    spread = (group == owner).astype(jnp.bfloat16)
    for f in range(frames):
        raised = exponents_ref[f].reshape(tokens, groups) + LEAST
        factor = (jnp.left_shift(1, raised).astype(jnp.float32) * 2.0**-LEAST).astype(jnp.bfloat16)
        factor = jnp.dot(factor, spread, preferred_element_type=jnp.float32)
        values = codes_ref[f].reshape(tokens, channels).astype(jnp.float32) * factor
        out_refs[f][...] = values.astype(jnp.bfloat16).reshape(rows, cols, channels)


def shifted_sum(sums):
    before, here, after = sums
    cols = here.shape[0]
    column = lax.broadcasted_iota(jnp.int32, here.shape, 0)
    before = jnp.where(column == 0, 0.0, pltpu.roll(before, 1, 0))
    after = jnp.where(column == cols - 1, 0.0, pltpu.roll(after, cols - 1, 0))
    return before + here + after


def add_taps(sums, slab, weights, a, b):
    for c in range(3):
        tap = (a * 3 + b) * 3 + c
        term = slab * weights[tap : tap + 1]
        sums[c] = term if sums[c] is None else sums[c] + term


def conv_own_kernel(before_ref, first_ref, second_ref, after_ref, weight_ref, out_ref):
    planes = (before_ref, first_ref, second_ref, after_ref)
    rows, cols, channels = first_ref.shape
    for start in range(0, channels, LANES):
        lanes = slice(start, start + LANES)
        weights = weight_ref[:, lanes]
        slabs = [[p[r, :, lanes].astype(jnp.float32) for r in range(rows)] for p in planes]
        for f in range(2):
            for r in range(rows):
                sums = [None] * 3
                for a in range(3):
                    for source in range(rows):
                        add_taps(sums, slabs[f + a][source], weights, a, source - r + 1)
                place = (f * rows + r) * cols
                out_ref[place : place + cols, lanes] = slabs[f + 1][r] + shifted_sum(sums)


def conv_edge_kernel(part_ref, above_ref, below_ref, weight_ref, out_ref):
    planes, cols, channels = above_ref.shape
    for start in range(0, channels, LANES):
        lanes = slice(start, start + LANES)
        weights = weight_ref[:, lanes]
        for r, ref, b in ((0, above_ref, 0), (1, below_ref, 2)):
            slabs = [ref[p, :, lanes].astype(jnp.float32) for p in range(planes)]
            for f in range(2):
                sums = [None] * 3
                for a in range(3):
                    add_taps(sums, slabs[f + a], weights, a, b)
                place = (f * 2 + r) * cols
                total = part_ref[place : place + cols, lanes] + shifted_sum(sums)
                out_ref[place : place + cols, lanes] = total.astype(jnp.bfloat16)


def neighbours(last, first, axis):
    size = lax.axis_size(axis)
    up = [(i, i + 1) for i in range(size - 1)]
    down = [(j, i) for i, j in up]
    return lax.ppermute(last, axis, up), lax.ppermute(first, axis, down)


def low_lanes(shape):
    return lax.broadcasted_iota(jnp.int32, shape, len(shape) - 1) < HEAD_DIM


def swap(x):
    return pltpu.roll(x, HEAD_DIM, x.ndim - 1)


def project_kernel(mixed_ref, shift_ref, scale_ref, wq_ref, wk_ref, wv_ref, out_ref):
    half = mixed_ref.shape[1] // 2
    parts = []
    for f in range(2):
        rows = pl.ds(f * half, half)
        x = jnp.concatenate([mixed_ref[0, rows, :], mixed_ref[1, rows, :]], axis=1)
        x = x.astype(jnp.float32)
        average = jnp.mean(x, axis=1, keepdims=True)
        centered = x - average
        variance = jnp.mean(centered * centered, axis=1, keepdims=True)
        x = centered * lax.rsqrt(variance + 1e-06)
        x = x * (1.0 + scale_ref[f : f + 1, :]) + shift_ref[f : f + 1, :]
        parts.append(x.astype(jnp.bfloat16))
    normed = jnp.concatenate(parts, axis=0)
    tokens = 2 * half
    low_all, low_half = low_lanes((tokens, LANES)), low_lanes((half, LANES))
    q, k, v = [
        jnp.dot(normed, w[...], preferred_element_type=jnp.float32)
        for w in (wq_ref, wk_ref, wv_ref)
    ]
    heads = wq_ref.shape[1] // HEAD_DIM
    for pair in range(heads // 2):
        lanes = slice(pair * LANES, (pair + 1) * LANES)
        qp, kp, vp = q[:, lanes], k[:, lanes], v[:, lanes]
        first, second = qp[:half], qp[half:]
        even, odd = 2 * pair, 2 * pair + 1
        out_ref[even, :tokens, :] = jnp.where(low_all, kp, swap(vp)).astype(jnp.bfloat16)
        out_ref[odd, :tokens, :] = jnp.where(low_all, swap(kp), vp).astype(jnp.bfloat16)
        out_ref[even, tokens:, :] = jnp.where(low_half, first, swap(second)).astype(jnp.bfloat16)
        out_ref[odd, tokens:, :] = jnp.where(low_half, swap(first), second).astype(jnp.bfloat16)
    for slot in range(heads, out_ref.shape[0]):
        out_ref[slot] = jnp.zeros(out_ref.shape[1:], jnp.bfloat16)


def query_rows(held_ref, start, step):
    tokens = held_ref.shape[1] * 2 // 3
    rows = step * (held_ref.shape[1] - tokens)
    packed = held_ref[start : start + step, tokens:, :].reshape(rows, LANES).astype(jnp.float32)
    low = low_lanes((rows, LANES))
    first = jnp.where(low, packed, 0.0)
    second = jnp.where(low, swap(packed), 0.0)
    return jnp.concatenate([first, second], axis=0).astype(jnp.bfloat16)


def scored(queries, kv):
    return lax.dot_general(
        queries, kv, (((1,), (1,)), ((), ())), preferred_element_type=jnp.float32
    )


def counted(kv):
    return jnp.where(low_lanes(kv.shape), jnp.ones_like(kv), kv)


FACTOR = LOG2E * HEAD_DIM ** (-0.5)


def copies_kernel(held_ref, out_ref):
    tokens = out_ref.shape[2]
    kv = held_ref[:, :tokens, :]
    for x in range(out_ref.shape[0]):
        out_ref[x] = kv


def attend_own_kernel(held_ref, top_ref, sum_ref):
    slots, width, _ = held_ref.shape
    tokens = width * 2 // 3
    kv = held_ref[:, :tokens, :].reshape(slots * tokens, LANES)
    values = counted(kv)
    step = slots // 2
    rows = step * tokens
    for start in range(0, slots, step):
        scores = scored(query_rows(held_ref, start, step), kv)
        top = jnp.max(scores, axis=1, keepdims=True)
        weights = jnp.exp2((scores - top) * FACTOR).astype(jnp.bfloat16)
        place = slice(start * tokens, start * tokens + rows)
        top_ref[place, :] = jnp.broadcast_to(top, (rows, LANES))
        sum_ref[place, :] = jnp.dot(weights, values, preferred_element_type=jnp.float32)


def attend_kernel(x_ref, held_ref, kv_ref, top_ref, sum_ref, out_ref):
    slots, width, _ = held_ref.shape
    tokens = width * 2 // 3
    half = tokens // 2
    others = [lax.rem(x_ref[0] + j, ROWS) for j in range(1, ROWS)]
    kv = jnp.concatenate([kv_ref[x].reshape(slots * tokens, LANES) for x in others], axis=0)
    values = counted(kv)
    step = slots // 2
    rows = step * tokens
    low = low_lanes((rows // 2, LANES))
    starts = list(range(0, slots, step))
    scores = scored(query_rows(held_ref, 0, step), kv)
    for start in starts:
        later = None
        if start != starts[-1]:
            later = scored(query_rows(held_ref, start + step, step), kv)
        place = slice(start * tokens, start * tokens + rows)
        own_top = top_ref[place, :][:, :1]
        top = jnp.maximum(jnp.max(scores, axis=1, keepdims=True), own_top)
        weights = jnp.exp2((scores - top) * FACTOR).astype(jnp.bfloat16)
        summed = jnp.dot(weights, values, preferred_element_type=jnp.float32)
        summed = summed + sum_ref[place, :] * jnp.exp2((own_top - top) * FACTOR)
        done = summed / swap(summed)
        result = jnp.where(low, swap(done[: rows // 2]), done[rows // 2 :])
        out_ref[start : start + step] = result.astype(jnp.bfloat16).reshape(step, half, LANES)
        scores = later


def unpack_kernel(in_ref, out_ref):
    half = in_ref.shape[1]
    low = low_lanes((half, LANES))
    for pair in range(out_ref.shape[2] // LANES):
        lanes = slice(pair * LANES, (pair + 1) * LANES)
        even = in_ref[2 * pair].astype(jnp.float32)
        odd = in_ref[2 * pair + 1].astype(jnp.float32)
        out_ref[0, :, lanes] = jnp.where(low, even, swap(odd)).astype(jnp.bfloat16)
        out_ref[1, :, lanes] = jnp.where(low, swap(even), odd).astype(jnp.bfloat16)


def call(kernel, shapes, *args, scalars=0):
    shapes = [jax.ShapeDtypeStruct(shape, kind) for shape, kind in shapes]
    in_specs = [pl.BlockSpec(memory_space=pltpu.SMEM)] * scalars
    in_specs += [pl.BlockSpec(memory_space=pltpu.VMEM)] * (len(args) - scalars)
    return pl.pallas_call(
        kernel,
        out_shape=shapes,
        in_specs=in_specs,
        out_specs=[pl.BlockSpec(memory_space=pltpu.VMEM)] * len(shapes),
        compiler_params=pltpu.CompilerParams(vmem_limit_bytes=48 * 1024 * 1024),
    )(*args)


def local(
    residual_codes,
    exponents,
    conv_weight,
    timestep,
    modulation,
    query_weight,
    key_weight,
    value_weight,
):
    frames, tile_rows, tile_cols, channels = residual_codes.shape
    local_width = query_weight.shape[1]
    tokens = frames * tile_rows * tile_cols
    half = tokens // 2
    narrow, wide = jnp.bfloat16, jnp.float32
    pair_index = lax.axis_index("tp")
    taps = lax.dynamic_slice_in_dim(conv_weight, pair_index * channels, channels, 3)
    taps = taps.reshape(27, channels).astype(wide)
    picked = jnp.take(modulation, timestep, axis=0).astype(wide)

    frame_shape = ((tile_rows, tile_cols, channels), narrow)
    first, second = call(dequantize_kernel, [frame_shape] * 2, residual_codes, exponents)
    before, after = neighbours(second, first, "frame")
    planes = (before, first, second, after)
    top_row = jnp.stack([p[0] for p in planes])
    bottom_row = jnp.stack([p[-1] for p in planes])
    above, below = neighbours(bottom_row, top_row, "patch")
    (part,) = call(conv_own_kernel, [((tokens, channels), wide)], *planes, taps)
    (mixed_half,) = call(
        conv_edge_kernel, [((tokens, channels), narrow)], part, above, below, taps
    )
    mixed = lax.all_gather(mixed_half, "tp", axis=0)
    (send,) = call(
        project_kernel,
        [((COLS, tokens + half, LANES), narrow)],
        mixed,
        picked[:, 0],
        picked[:, 1],
        query_weight,
        key_weight,
        value_weight,
    )
    held = lax.all_to_all(send, "patch", 0, 0, axis_index_groups=Y_GROUPS)
    (copies,) = call(copies_kernel, [((ROWS, COLS, tokens, LANES), narrow)], held)
    kv = lax.all_to_all(copies, "patch", 0, 0, axis_index_groups=X_GROUPS)
    partial = ((COLS * tokens, LANES), wide)
    top, summed = call(attend_own_kernel, [partial] * 2, held)
    x_index = (lax.axis_index("patch") // COLS).reshape(1)
    (result,) = call(
        attend_kernel,
        [((COLS, half, LANES), narrow)],
        x_index,
        held,
        kv,
        top,
        summed,
        scalars=1,
    )
    back = lax.all_to_all(result, "patch", 0, 0, axis_index_groups=Y_GROUPS)
    (out,) = call(unpack_kernel, [((frames, half, local_width), narrow)], back)
    return out.reshape(frames, tile_rows, tile_cols, local_width)


def solution(mesh):
    in_specs = (
        P("frame", "patch", None, "tp"),
        P("frame", "patch", None, "tp"),
        P(),
        P("frame"),
        P(),
        P(None, "tp"),
        P(None, "tp"),
        P(None, "tp"),
    )
    out_specs = P("frame", "patch", None, "tp")
    return jax.shard_map(local, mesh=mesh, in_specs=in_specs, out_specs=out_specs, check_vma=False)
```

time: 94.3 us -> 91.4 us (0.969)
  waiting for transfers between devices: 24.9 us -> 21.3 us
  Pallas kernels: 7.48 us -> 10.1 us
  other arithmetic: 2.91 us -> 1.49 us
    pallas_call x3 -> x8, Pallas kernels: 7.48 us -> 10.1 us  [call(): pl.pallas_call(kernel, out_shape=shapes, in_specs=in_specs, out_specs=[pl...]
    all_to_all x1, waiting for transfers between devices: 16.1 us -> 14.1 us  [local(): kv = lax.all_to_all(copies, 'patch', 0, 0, axis_index_groups=X_GROUPS)]
    ppermute x4, waiting for transfers between devices: 8.84 us -> 7.16 us  [neighbours(): return (lax.ppermute(last, axis, up), lax.ppermute(first, axis, down))]
    unnamed x14 -> x13, local copies, waits for them, and re-layouts: 0.39 us -> 1.9 us
    broadcast_in_dim x1 -> x0, local copies, waits for them, and re-layouts: 1.23 us -> none  [local(): jnp.broadcast_to(held[None, :, :tokens], (ROWS, COLS, tokens, LANES))]
    convert_element_type x3 -> x2, other arithmetic: 1.31 us -> 0.1 us  [the longest x1 0.08 us: local(): picked = jnp.take(modulation, timestep, axis=0).astype(wide)]
  transfers between devices with their start and end apart: 5 -> 5, of which waited for: 4 -> 4; matrix products, arithmetic and copies ran while one was open for 1% -> 2% of each run, Pallas kernels for 0% -> 3%
where the time goes in v3:
time: 91.4 us; the launch traced here: 91.1 us
  blocking collectives  39.7 us (43%)
  waiting for transfers between devices  21.3 us (23%)
  starting transfers between devices  15.7 us (17%)
  Pallas kernels  10.1 us (11%)
  local copies, waits for them, and re-layouts  2.57 us (3%)
  other arithmetic  1.49 us (2%)
    all_to_all x1, blocking collectives, local(): held = lax.all_to_all(send, 'patch', 0, 0, axis_index_groups=Y_GROUPS)  21.3 us
    all_to_all x1, waiting for transfers between devices, local(): kv = lax.all_to_all(copies, 'patch', 0, 0, axis_index_groups=X_GROUPS)  14.1 us
    all_to_all x1, blocking collectives, local(): back = lax.all_to_all(result, 'patch', 0, 0, axis_index_groups=Y_GROUPS)  12.1 us
    ppermute x4, starting transfers between devices, neighbours(): return (lax.ppermute(last, axis, up), lax.ppermute(first, axis, down))  11.4 us
    pallas_call x8, Pallas kernels, call(): pl.pallas_call(kernel, out_shape=shapes, in_specs=in_specs, out_specs=[pl...  10.1 us
    ppermute x4, waiting for transfers between devices, neighbours(): return (lax.ppermute(last, axis, up), lax.ppermute(first, axis, down))  7.16 us
    all_gather x1, blocking collectives, local(): mixed = lax.all_gather(mixed_half, 'tp', axis=0)  6.35 us
    all_to_all x1, starting transfers between devices, local(): kv = lax.all_to_all(copies, 'patch', 0, 0, axis_index_groups=X_GROUPS)  4.3 us
  transfers between devices with their start and end apart: 5, of which 4 were waited for; matrix products, arithmetic and copies ran while one was open for 2% of the time, Pallas kernels for 3%

profile of v3, /device:TPU:128, one launch (start us, length us, event | category | flops | bytes accessed | tf_op | source)
XLA Modules:
  0.0 91.1 jit_solution(6638081340631052625)
XLA Ops:
  0.0 0.0 copy-start
  0.0 0.9 copy.10.exponents_ref
  0.9 1.0 %copy-done.4 = s32[2,2,32,768]{3,2,1,0:T(8,128)S(1)} copy-done((s32[2,2,32,768]{3,2,1,0:T(8,128)S(1)}, s32[2,2,32,768]{3,2,1,0:T(8,128)}, u32[]{:S(2)}) %copy-start.4) | copy-done | bytes 393240
  1.9 0.2 shard_map.82
  2.1 1.9 %collective-permute-start = (bf16[2,32,768]{2,1,0:T(8,128)(2,1)S(1)}, bf16[2,32,768]{2,1,0:T(8,128)(2,1)S(1)}, u32[]{:S(2)}, u32[]{:S(2)}) collective-permute-start(bf16[2,32,768]{2,1,0:T(8,128)(2,1)S(1)} %get-tuple-element.9.second_ref), channel_id=1, source_target_pairs={{0,64},{64,128},{128,192},{192,256},{256,320},{320,384},{384,448},... | collective-permute-start | bytes 294920 | tf_op jit(solution)/shard_map/ppermute | solution.py:89
  4.0 4.5 %collective-permute-start.1 = (bf16[2,32,768]{2,1,0:T(8,128)(2,1)S(1)}, bf16[2,32,768]{2,1,0:T(8,128)(2,1)S(1)}, u32[]{:S(2)}, u32[]{:S(2)}) collective-permute-start(bf16[2,32,768]{2,1,0:T(8,128)(2,1)S(1)} %get-tuple-element.10.first_ref), channel_id=1, source_target_pairs={{64,0},{128,64},{192,128},{256,192},{320,256},{384,320},{448,384},... | collective-permute-start | bytes 294920 | tf_op jit(solution)/shard_map/ppermute | solution.py:89
  8.6 0.7 compare_and_fusion
  9.2 0.7 compare_select_fusion
  9.9 0.6 gather_fusion
  10.5 0.1 fusion
  10.6 0.0 collective-permute-done.before_ref
  10.6 1.6 %collective-permute-done.1.after_ref = bf16[2,32,768]{2,1,0:T(8,128)(2,1)S(1)} collective-permute-done((bf16[2,32,768]{2,1,0:T(8,128)(2,1)S(1)}, bf16[2,32,768]{2,1,0:T(8,128)(2,1)S(1)}, u32[]{:S(2)}, u32[]{:S(2)}) %collective-permute-start.1) | collective-permute-done | bytes 98336 | tf_op jit(solution)/shard_map/ppermute | solution.py:89
  12.2 0.0 copy-start.3
  12.3 3.6 %collective-permute-start.2 = (bf16[4,32,768]{2,1,0:T(8,128)(2,1)S(1)}, bf16[4,32,768]{2,1,0:T(8,128)(2,1)S(1)}, u32[]{:S(2)}, u32[]{:S(2)}) collective-permute-start(bf16[4,32,768]{2,1,0:T(8,128)(2,1)S(1)} %pad_maximum_fusion), channel_id=1, source_target_pairs={{0,2},{2,4},{4,6},{6,8},{8,10},{10,12},{12,14},{14,16},{16,18},{18... | collective-permute-start | bytes 589832 | tf_op jit(solution)/shard_map/ppermute | solution.py:89
  15.9 1.3 %collective-permute-start.3 = (bf16[4,32,768]{2,1,0:T(8,128)(2,1)S(1)}, bf16[4,32,768]{2,1,0:T(8,128)(2,1)S(1)}, u32[]{:S(2)}, u32[]{:S(2)}) collective-permute-start(bf16[4,32,768]{2,1,0:T(8,128)(2,1)S(1)} %pad_maximum_fusion.1), channel_id=1, source_target_pairs={{2,0},{4,2},{6,4},{8,6},{10,8},{12,10},{14,12},{16,14},{18,16},{20... | collective-permute-start | bytes 589832 | tf_op jit(solution)/shard_map/ppermute | solution.py:89
  17.3 0.0 copy-start.1
  17.3 0.0 copy-start.2
  17.4 0.6 shard_map.83.part_ref
  17.9 1.1 %collective-permute-done.2.above_ref = bf16[4,32,768]{2,1,0:T(8,128)(2,1)S(1)} collective-permute-done((bf16[4,32,768]{2,1,0:T(8,128)(2,1)S(1)}, bf16[4,32,768]{2,1,0:T(8,128)(2,1)S(1)}, u32[]{:S(2)}, u32[]{:S(2)}) %collective-permute-start.2) | collective-permute-done | bytes 196640 | tf_op jit(solution)/shard_map/ppermute | solution.py:89
  19.0 4.4 %collective-permute-done.3.below_ref = bf16[4,32,768]{2,1,0:T(8,128)(2,1)S(1)} collective-permute-done((bf16[4,32,768]{2,1,0:T(8,128)(2,1)S(1)}, bf16[4,32,768]{2,1,0:T(8,128)(2,1)S(1)}, u32[]{:S(2)}, u32[]{:S(2)}) %collective-permute-start.3) | collective-permute-done | bytes 196640 | tf_op jit(solution)/shard_map/ppermute | solution.py:89
  23.5 0.3 shard_map.84
  23.8 6.3 %all-gather = bf16[256,768]{1,0:T(8,128)(2,1)S(1)} all-gather(bf16[128,768]{1,0:T(8,128)(2,1)S(1)} %shard_map.84), channel_id=2, replica_groups=mesh['frame'=8,'patch'=32,'tp'=2] {'tp'}, dimensions={0}, use_global_device_ids=true | all-gather | bytes 589824 | tf_op jit(solution)/shard_map/all_gather | solution.py:263
  30.2 0.0 copy-done.3
  30.2 1.1 %shard_map.85 = bf16[8,192,128]{2,1,0:T(8,128)(2,1)S(1)} custom-call(bf16[2,128,768]{2,1,0:T(8,128)(2,1)S(1)} %bitcast.7, f32[2,1536]{1,0:T(2,128)S(1)} %get-tuple-element.22.shift_ref, f32[2,1536]{1,0:T(2,128)S(1)} %get-tuple-element.21.scale_ref, bf16[1536,384]{1,0:T(8,128)(2,1)S(1)} %copy-done.1, bf16[1536,384]{1,0:T(8,128)(2,1)S(1)} %copy-done.2, ...), custom_call_target="tpu_custom_call" | custom-call | tf_op jit(solution)/shard_map/pallas_call | solution.py:223
  31.3 21.3 %all_to_all.15.held_ref = bf16[8,192,128]{2,1,0:T(8,128)(2,1)S(1)} all-to-all(bf16[8,192,128]{2,1,0:T(8,128)(2,1)S(1)} %shard_map.85), channel_id=1, replica_groups={{0,2,4,6,8,10,12,14},{16,18,20,22,24,26,28,30},{32,34,36,38,40,42,44,46..., dimensions={0} | all-to-all | bytes 786432 | tf_op jit(solution)/shard_map/all_to_all | solution.py:274
  52.6 1.1 %shard_map.86 = bf16[4,8,128,128]{3,2,1,0:T(8,128)(2,1)} custom-call(bf16[8,192,128]{2,1,0:T(8,128)(2,1)S(1)} %all_to_all.15.held_ref), custom_call_target="tpu_custom_call" | custom-call | tf_op jit(solution)/shard_map/pallas_call | solution.py:223
  53.7 4.3 %all-to-all-start.1 = ((bf16[4,8,128,128]{3,2,1,0:T(8,128)(2,1)}), bf16[4,8,128,128]{3,2,1,0:T(8,128)(2,1)S(1)}, u32[]{:S(2)}, u32[]{:S(2)}) async-start(bf16[4,8,128,128]{3,2,1,0:T(8,128)(2,1)} %shard_map.86), calls=%async_computation.1 | async-start | bytes 2097152 | tf_op jit(solution)/shard_map/all_to_all | solution.py:276
  58.0 2.0 %shard_map.87 = (f32[1024,128]{1,0:T(8,128)S(1)}, f32[1024,128]{1,0:T(8,128)S(1)}) custom-call(bf16[8,192,128]{2,1,0:T(8,128)(2,1)S(1)} %all_to_all.15.held_ref), custom_call_target="tpu_custom_call" | custom-call | tf_op jit(solution)/shard_map/pallas_call | solution.py:223
  60.0 14.1 %all-to-all-done.1.kv_ref = bf16[4,8,128,128]{3,2,1,0:T(8,128)(2,1)S(1)} async-done(((bf16[4,8,128,128]{3,2,1,0:T(8,128)(2,1)}), bf16[4,8,128,128]{3,2,1,0:T(8,128)(2,1)S(1)}, u32[]{:S(2)}, u32[]{:S(2)}) %all-to-all-start.1) | async-done | bytes 1048608 | tf_op jit(solution)/shard_map/all_to_all | solution.py:276
  74.1 4.0 %shard_map.88 = bf16[8,64,128]{2,1,0:T(8,128)(2,1)S(1)} custom-call(s32[1]{0:T(128)} %bitcast.x_ref, bf16[8,192,128]{2,1,0:T(8,128)(2,1)S(1)} %all_to_all.15.held_ref, bf16[4,8,128,128]{3,2,1,0:T(8,128)(2,1)S(1)} %all-to-all-done.1.kv_ref, f32[1024,128]{1,0:T(8,128)S(1)} %get-tuple-element.11.top_ref, f32[1024,128]{1,0:T(8,128)S(1)} %get-tuple-element.12.sum_ref), custom_call_target="tpu_custom_call" | custom-call | tf_op jit(solution)/shard_map/pallas_call | solution.py:223
  78.2 12.1 %all_to_all.16.in_ref = bf16[8,64,128]{2,1,0:T(8,128)(2,1)S(1)} all-to-all(bf16[8,64,128]{2,1,0:T(8,128)(2,1)S(1)} %shard_map.88), channel_id=1, replica_groups={{0,2,4,6,8,10,12,14},{16,18,20,22,24,26,28,30},{32,34,36,38,40,42,44,46..., dimensions={0} | all-to-all | bytes 262144 | tf_op jit(solution)/shard_map/all_to_all | solution.py:290
  90.3 0.7 shard_map.89
  (15 shorter events, 0.2 us)
Async XLA Ops:
  0.0 9.9 %copy-start = (bf16[50,2,1536]{2,1,0:T(2,128)(2,1)S(1)}, bf16[50,2,1536]{2,1,0:T(2,128)(2,1)}, u32[]{:S(2)}) copy-start(bf16[50,2,1536]{2,1,0:T(2,128)(2,1)} %param.12) | copy-start | bytes 921604
  0.9 1.0 %copy-start.4 = (s32[2,2,32,768]{3,2,1,0:T(8,128)S(1)}, s32[2,2,32,768]{3,2,1,0:T(8,128)}, u32[]{:S(2)}) copy-start(s32[2,2,32,768]{3,2,1,0:T(8,128)} %codes_ref.1) | copy-start | bytes 1179652
  1.9 15.4 %copy-start.5 = (bf16[3,3,3,1536]{3,2,1,0:T(4,128)(2,1)S(1)}, bf16[3,3,3,1536]{3,2,1,0:T(4,128)(2,1)}, u32[]{:S(2)}) copy-start(bf16[3,3,3,1536]{3,2,1,0:T(4,128)(2,1)} %param.10) | copy-start | bytes 248836
  2.1 8.5 %collective-permute-start = (bf16[2,32,768]{2,1,0:T(8,128)(2,1)S(1)}, bf16[2,32,768]{2,1,0:T(8,128)(2,1)S(1)}, u32[]{:S(2)}, u32[]{:S(2)}) collective-permute-start(bf16[2,32,768]{2,1,0:T(8,128)(2,1)S(1)} %get-tuple-element.9.second_ref), channel_id=1, source_target_pairs={{0,64},{64,128},{128,192},{192,256},{256,320},{320,384},{384,448},... | collective-permute-start | bytes 294920 | tf_op jit(solution)/shard_map/ppermute | solution.py:89
  4.0 8.2 %collective-permute-start.1 = (bf16[2,32,768]{2,1,0:T(8,128)(2,1)S(1)}, bf16[2,32,768]{2,1,0:T(8,128)(2,1)S(1)}, u32[]{:S(2)}, u32[]{:S(2)}) collective-permute-start(bf16[2,32,768]{2,1,0:T(8,128)(2,1)S(1)} %get-tuple-element.10.first_ref), channel_id=1, source_target_pairs={{64,0},{128,64},{192,128},{256,192},{320,256},{384,320},{448,384},... | collective-permute-start | bytes 294920 | tf_op jit(solution)/shard_map/ppermute | solution.py:89
  12.2 18.0 %copy-start.3 = (bf16[1536,384]{1,0:T(8,128)(2,1)S(1)}, bf16[1536,384]{1,0:T(8,128)(2,1)}, u32[]{:S(2)}) copy-start(bf16[1536,384]{1,0:T(8,128)(2,1)} %wv_ref.1) | copy-start | bytes 3538948
  12.3 6.8 %collective-permute-start.2 = (bf16[4,32,768]{2,1,0:T(8,128)(2,1)S(1)}, bf16[4,32,768]{2,1,0:T(8,128)(2,1)S(1)}, u32[]{:S(2)}, u32[]{:S(2)}) collective-permute-start(bf16[4,32,768]{2,1,0:T(8,128)(2,1)S(1)} %pad_maximum_fusion), channel_id=1, source_target_pairs={{0,2},{2,4},{4,6},{6,8},{8,10},{10,12},{12,14},{14,16},{16,18},{18... | collective-permute-start | bytes 589832 | tf_op jit(solution)/shard_map/ppermute | solution.py:89
  15.9 7.6 %collective-permute-start.3 = (bf16[4,32,768]{2,1,0:T(8,128)(2,1)S(1)}, bf16[4,32,768]{2,1,0:T(8,128)(2,1)S(1)}, u32[]{:S(2)}, u32[]{:S(2)}) collective-permute-start(bf16[4,32,768]{2,1,0:T(8,128)(2,1)S(1)} %pad_maximum_fusion.1), channel_id=1, source_target_pairs={{2,0},{4,2},{6,4},{8,6},{10,8},{12,10},{14,12},{16,14},{18,16},{20... | collective-permute-start | bytes 589832 | tf_op jit(solution)/shard_map/ppermute | solution.py:89
  17.3 12.9 %copy-start.1 = (bf16[1536,384]{1,0:T(8,128)(2,1)S(1)}, bf16[1536,384]{1,0:T(8,128)(2,1)}, u32[]{:S(2)}) copy-start(bf16[1536,384]{1,0:T(8,128)(2,1)} %wq_ref.1) | copy-start | bytes 3538948
  17.3 12.8 %copy-start.2 = (bf16[1536,384]{1,0:T(8,128)(2,1)S(1)}, bf16[1536,384]{1,0:T(8,128)(2,1)}, u32[]{:S(2)}) copy-start(bf16[1536,384]{1,0:T(8,128)(2,1)} %wk_ref.1) | copy-start | bytes 3538948
  53.7 20.4 %all-to-all-start.1 = ((bf16[4,8,128,128]{3,2,1,0:T(8,128)(2,1)}), bf16[4,8,128,128]{3,2,1,0:T(8,128)(2,1)S(1)}, u32[]{:S(2)}, u32[]{:S(2)}) async-start(bf16[4,8,128,128]{3,2,1,0:T(8,128)(2,1)} %shard_map.86), calls=%async_computation.1 | async-start | bytes 2097152 | tf_op jit(solution)/shard_map/all_to_all | solution.py:276

commit v4 on v3

--- a/solution.py
+++ b/solution.py
@@ -18,19 +18,34 @@
 LEAST = 16
 
 
-def dequantize_kernel(codes_ref, exponents_ref, *out_refs):
-    frames, rows, cols, channels = codes_ref.shape
-    groups = exponents_ref.shape[-1]
-    tokens = rows * cols
+def dequantize_kernel(codes_ref, exponents_ref, first_ref, second_ref, codes, exps, sems):
+    frames, rows, cols, channels = codes.shape
+    groups = exps.shape[1]
+    small = pltpu.make_async_copy(exponents_ref, exps, sems.at[frames * rows])
+    small.start()
+    copies = []
+    for f in range(frames):
+        for r in range(rows):
+            place = f * rows + r
+            copy = pltpu.make_async_copy(codes_ref.at[f, r], codes.at[f, r], sems.at[place])
+            copy.start()
+            copies.append(copy)
     group = lax.broadcasted_iota(jnp.int32, (groups, channels), 0)
     owner = lax.broadcasted_iota(jnp.int32, (groups, channels), 1) // BLOCK
     spread = (group == owner).astype(jnp.bfloat16)
-    for f in range(frames):
-        raised = exponents_ref[f].reshape(tokens, groups) + LEAST
-        factor = (jnp.left_shift(1, raised).astype(jnp.float32) * 2.0**-LEAST).astype(jnp.bfloat16)
-        factor = jnp.dot(factor, spread, preferred_element_type=jnp.float32)
-        values = codes_ref[f].reshape(tokens, channels).astype(jnp.float32) * factor
-        out_refs[f][...] = values.astype(jnp.bfloat16).reshape(rows, cols, channels)
+    small.wait()
+    for f, out_ref in enumerate((first_ref, second_ref)):
+        for r in range(rows):
+            raised = exps[f, :, r, :] + LEAST
+            factor = jnp.left_shift(1, raised).astype(jnp.float32) * 2.0**-LEAST
+            factor = lax.dot_general(
+                factor.astype(jnp.bfloat16),
+                spread,
+                (((0,), (0,)), ((), ())),
+                preferred_element_type=jnp.float32,
+            )
+            copies[f * rows + r].wait()
+            out_ref[r] = (codes[f, r].astype(jnp.float32) * factor).astype(jnp.bfloat16)
 
 
 def shifted_sum(sums):
@@ -97,7 +112,7 @@
     return pltpu.roll(x, HEAD_DIM, x.ndim - 1)
 
 
-def project_kernel(mixed_ref, shift_ref, scale_ref, wq_ref, wk_ref, wv_ref, out_ref):
+def project_kernel(step_ref, mixed_ref, modulation_ref, wq_ref, wk_ref, wv_ref, out_ref):
     half = mixed_ref.shape[1] // 2
     parts = []
     for f in range(2):
@@ -108,7 +123,8 @@
         centered = x - average
         variance = jnp.mean(centered * centered, axis=1, keepdims=True)
         x = centered * lax.rsqrt(variance + 1e-06)
-        x = x * (1.0 + scale_ref[f : f + 1, :]) + shift_ref[f : f + 1, :]
+        picked = modulation_ref[step_ref[f]].astype(jnp.float32)
+        x = x * (1.0 + picked[1:2]) + picked[0:1]
         parts.append(x.astype(jnp.bfloat16))
     normed = jnp.concatenate(parts, axis=0)
     tokens = 2 * half
@@ -154,11 +170,16 @@
 FACTOR = LOG2E * HEAD_DIM ** (-0.5)
 
 
-def copies_kernel(held_ref, out_ref):
+def copies_kernel(held_ref, out_ref, sems):
     tokens = out_ref.shape[2]
-    kv = held_ref[:, :tokens, :]
-    for x in range(out_ref.shape[0]):
-        out_ref[x] = kv
+    copies = [
+        pltpu.make_async_copy(held_ref.at[:, pl.ds(0, tokens), :], out_ref.at[x], sems.at[x])
+        for x in range(out_ref.shape[0])
+    ]
+    for copy in copies:
+        copy.start()
+    for copy in copies:
+        copy.wait()
 
 
 def attend_own_kernel(held_ref, top_ref, sum_ref):
@@ -216,15 +237,19 @@
         out_ref[1, :, lanes] = jnp.where(low, swap(even), odd).astype(jnp.bfloat16)
 
 
-def call(kernel, shapes, *args, scalars=0):
+SMEM = pl.BlockSpec(memory_space=pltpu.SMEM)
+VMEM = pl.BlockSpec(memory_space=pltpu.VMEM)
+HBM = pl.BlockSpec(memory_space=pltpu.HBM)
+
+
+def call(kernel, shapes, *args, spaces=None, out_space=VMEM, scratch=()):
     shapes = [jax.ShapeDtypeStruct(shape, kind) for shape, kind in shapes]
-    in_specs = [pl.BlockSpec(memory_space=pltpu.SMEM)] * scalars
-    in_specs += [pl.BlockSpec(memory_space=pltpu.VMEM)] * (len(args) - scalars)
     return pl.pallas_call(
         kernel,
         out_shape=shapes,
-        in_specs=in_specs,
-        out_specs=[pl.BlockSpec(memory_space=pltpu.VMEM)] * len(shapes),
+        in_specs=spaces or [VMEM] * len(args),
+        out_specs=[out_space] * len(shapes),
+        scratch_shapes=scratch,
         compiler_params=pltpu.CompilerParams(vmem_limit_bytes=48 * 1024 * 1024),
     )(*args)
 
@@ -247,10 +272,21 @@
     pair_index = lax.axis_index("tp")
     taps = lax.dynamic_slice_in_dim(conv_weight, pair_index * channels, channels, 3)
     taps = taps.reshape(27, channels).astype(wide)
-    picked = jnp.take(modulation, timestep, axis=0).astype(wide)
 
     frame_shape = ((tile_rows, tile_cols, channels), narrow)
-    first, second = call(dequantize_kernel, [frame_shape] * 2, residual_codes, exponents)
+    by_group = exponents.transpose(0, 3, 1, 2)
+    first, second = call(
+        dequantize_kernel,
+        [frame_shape] * 2,
+        pltpu.with_memory_space_constraint(residual_codes, pltpu.HBM),
+        pltpu.with_memory_space_constraint(by_group, pltpu.HBM),
+        spaces=[HBM, HBM],
+        scratch=[
+            pltpu.VMEM(residual_codes.shape, jnp.int32),
+            pltpu.VMEM(by_group.shape, jnp.int32),
+            pltpu.SemaphoreType.DMA((frames * tile_rows + 1,)),
+        ],
+    )
     before, after = neighbours(second, first, "frame")
     planes = (before, first, second, after)
     top_row = jnp.stack([p[0] for p in planes])
@@ -264,15 +300,22 @@
     (send,) = call(
         project_kernel,
         [((COLS, tokens + half, LANES), narrow)],
+        timestep,
         mixed,
-        picked[:, 0],
-        picked[:, 1],
+        modulation,
         query_weight,
         key_weight,
         value_weight,
+        spaces=[SMEM] + [VMEM] * 5,
     )
     held = lax.all_to_all(send, "patch", 0, 0, axis_index_groups=Y_GROUPS)
-    (copies,) = call(copies_kernel, [((ROWS, COLS, tokens, LANES), narrow)], held)
+    (copies,) = call(
+        copies_kernel,
+        [((ROWS, COLS, tokens, LANES), narrow)],
+        held,
+        out_space=HBM,
+        scratch=[pltpu.SemaphoreType.DMA((ROWS,))],
+    )
     kv = lax.all_to_all(copies, "patch", 0, 0, axis_index_groups=X_GROUPS)
     partial = ((COLS * tokens, LANES), wide)
     top, summed = call(attend_own_kernel, [partial] * 2, held)
@@ -285,7 +328,7 @@
         kv,
         top,
         summed,
-        scalars=1,
+        spaces=[SMEM] + [VMEM] * 4,
     )
     back = lax.all_to_all(result, "patch", 0, 0, axis_index_groups=Y_GROUPS)
     (out,) = call(unpack_kernel, [((frames, half, local_width), narrow)], back)

time: 91.4 us -> 91.4 us (level)
  local copies, waits for them, and re-layouts: 2.57 us -> 0.11 us
  waiting for transfers between devices: 21.3 us -> 23.4 us
  Pallas kernels: 10.1 us -> 11.8 us
  other arithmetic: 1.49 us -> 0.07 us
    ppermute x4, waiting for transfers between devices: 7.16 us -> 9.19 us  [neighbours(): return (lax.ppermute(last, axis, up), lax.ppermute(first, axis, down))]
    unnamed x13 -> x12, local copies, waits for them, and re-layouts: 1.9 us -> 0.03 us
    pallas_call x8, Pallas kernels: 10.1 us -> 11.8 us  [call(): pl.pallas_call(kernel, out_shape=shapes, in_specs=spaces or [VMEM] * len(...]
  transfers between devices with their start and end apart: 5 -> 5, of which waited for: 4 -> 5; matrix products, arithmetic and copies ran while one was open for 2% -> 0% of each run, Pallas kernels for 3% -> 3%
where the time goes in v4:
time: 91.4 us; the launch traced here: 91 us
  blocking collectives  39.7 us (43%)
  waiting for transfers between devices  23.4 us (26%)
  starting transfers between devices  15.7 us (17%)
  Pallas kernels  11.8 us (13%)
    all_to_all x1, blocking collectives, local(): held = lax.all_to_all(send, 'patch', 0, 0, axis_index_groups=Y_GROUPS)  21.3 us
    all_to_all x1, waiting for transfers between devices, local(): kv = lax.all_to_all(copies, 'patch', 0, 0, axis_index_groups=X_GROUPS)  14.2 us
    all_to_all x1, blocking collectives, local(): back = lax.all_to_all(result, 'patch', 0, 0, axis_index_groups=Y_GROUPS)  12.1 us
    pallas_call x8, Pallas kernels, call(): pl.pallas_call(kernel, out_shape=shapes, in_specs=spaces or [VMEM] * len(...  11.8 us
    ppermute x4, starting transfers between devices, neighbours(): return (lax.ppermute(last, axis, up), lax.ppermute(first, axis, down))  11.4 us
    ppermute x4, waiting for transfers between devices, neighbours(): return (lax.ppermute(last, axis, up), lax.ppermute(first, axis, down))  9.19 us
    all_gather x1, blocking collectives, local(): mixed = lax.all_gather(mixed_half, 'tp', axis=0)  6.35 us
    all_to_all x1, starting transfers between devices, local(): kv = lax.all_to_all(copies, 'patch', 0, 0, axis_index_groups=X_GROUPS)  4.32 us
  transfers between devices with their start and end apart: 5, of which 5 were waited for; matrix products, arithmetic and copies ran while one was open for 0% of the time, Pallas kernels for 3%

profile of v4, /device:TPU:128, one launch (start us, length us, event | category | flops | bytes accessed | tf_op | source)
XLA Modules:
  0.0 91.0 jit_solution(5049465090731149330)
XLA Ops:
  0.0 0.0 copy-start.5
  0.0 1.7 %shard_map.82 = (bf16[2,32,768]{2,1,0:T(8,128)(2,1)S(1)}, bf16[2,32,768]{2,1,0:T(8,128)(2,1)S(1)}) custom-call(s32[2,2,32,768]{3,2,1,0:T(8,128)} %codes_ref.1, s32[2,12,2,32]{3,2,1,0:T(2,128)} %bitcast.5), custom_call_target="tpu_custom_call" | custom-call | tf_op jit(solution)/shard_map/pallas_call | solution.py:247
  1.7 1.9 %collective-permute-start = (bf16[2,32,768]{2,1,0:T(8,128)(2,1)S(1)}, bf16[2,32,768]{2,1,0:T(8,128)(2,1)S(1)}, u32[]{:S(2)}, u32[]{:S(2)}) collective-permute-start(bf16[2,32,768]{2,1,0:T(8,128)(2,1)S(1)} %get-tuple-element.9.second_ref), channel_id=1, source_target_pairs={{0,64},{64,128},{128,192},{192,256},{256,320},{320,384},{384,448},... | collective-permute-start | bytes 294920 | tf_op jit(solution)/shard_map/ppermute | solution.py:104
  3.6 4.5 %collective-permute-start.1 = (bf16[2,32,768]{2,1,0:T(8,128)(2,1)S(1)}, bf16[2,32,768]{2,1,0:T(8,128)(2,1)S(1)}, u32[]{:S(2)}, u32[]{:S(2)}) collective-permute-start(bf16[2,32,768]{2,1,0:T(8,128)(2,1)S(1)} %get-tuple-element.10.first_ref), channel_id=1, source_target_pairs={{64,0},{128,64},{192,128},{256,192},{320,256},{384,320},{448,384},... | collective-permute-start | bytes 294920 | tf_op jit(solution)/shard_map/ppermute | solution.py:104
  8.2 0.3 collective-permute-done.before_ref
  8.5 3.3 %collective-permute-done.1.after_ref = bf16[2,32,768]{2,1,0:T(8,128)(2,1)S(1)} collective-permute-done((bf16[2,32,768]{2,1,0:T(8,128)(2,1)S(1)}, bf16[2,32,768]{2,1,0:T(8,128)(2,1)S(1)}, u32[]{:S(2)}, u32[]{:S(2)}) %collective-permute-start.1) | collective-permute-done | bytes 98336 | tf_op jit(solution)/shard_map/ppermute | solution.py:104
  11.8 0.0 copy-start.2
  11.9 3.6 %collective-permute-start.2 = (bf16[4,32,768]{2,1,0:T(8,128)(2,1)S(1)}, bf16[4,32,768]{2,1,0:T(8,128)(2,1)S(1)}, u32[]{:S(2)}, u32[]{:S(2)}) collective-permute-start(bf16[4,32,768]{2,1,0:T(8,128)(2,1)S(1)} %pad_maximum_fusion), channel_id=1, source_target_pairs={{0,2},{2,4},{4,6},{6,8},{8,10},{10,12},{12,14},{14,16},{16,18},{18... | collective-permute-start | bytes 589832 | tf_op jit(solution)/shard_map/ppermute | solution.py:104
  15.5 1.3 %collective-permute-start.3 = (bf16[4,32,768]{2,1,0:T(8,128)(2,1)S(1)}, bf16[4,32,768]{2,1,0:T(8,128)(2,1)S(1)}, u32[]{:S(2)}, u32[]{:S(2)}) collective-permute-start(bf16[4,32,768]{2,1,0:T(8,128)(2,1)S(1)} %pad_maximum_fusion.1), channel_id=1, source_target_pairs={{2,0},{4,2},{6,4},{8,6},{10,8},{12,10},{14,12},{16,14},{18,16},{20... | collective-permute-start | bytes 589832 | tf_op jit(solution)/shard_map/ppermute | solution.py:104
  16.8 0.0 copy-done.5
  16.9 0.0 copy-start
  16.9 0.0 copy-start.1
  16.9 0.0 copy-start.4
  17.0 0.6 shard_map.83.part_ref
  17.5 1.1 %collective-permute-done.2.above_ref = bf16[4,32,768]{2,1,0:T(8,128)(2,1)S(1)} collective-permute-done((bf16[4,32,768]{2,1,0:T(8,128)(2,1)S(1)}, bf16[4,32,768]{2,1,0:T(8,128)(2,1)S(1)}, u32[]{:S(2)}, u32[]{:S(2)}) %collective-permute-start.2) | collective-permute-done | bytes 196640 | tf_op jit(solution)/shard_map/ppermute | solution.py:104
  18.6 4.4 %collective-permute-done.3.below_ref = bf16[4,32,768]{2,1,0:T(8,128)(2,1)S(1)} collective-permute-done((bf16[4,32,768]{2,1,0:T(8,128)(2,1)S(1)}, bf16[4,32,768]{2,1,0:T(8,128)(2,1)S(1)}, u32[]{:S(2)}, u32[]{:S(2)}) %collective-permute-start.3) | collective-permute-done | bytes 196640 | tf_op jit(solution)/shard_map/ppermute | solution.py:104
  23.1 0.3 shard_map.84
  23.4 6.3 %all-gather = bf16[256,768]{1,0:T(8,128)(2,1)S(1)} all-gather(bf16[128,768]{1,0:T(8,128)(2,1)S(1)} %shard_map.84), channel_id=2, replica_groups=mesh['frame'=8,'patch'=32,'tp'=2] {'tp'}, dimensions={0}, use_global_device_ids=true | all-gather | bytes 589824 | tf_op jit(solution)/shard_map/all_gather | solution.py:299
  29.8 0.0 copy-done.3
  29.8 0.0 copy-done.2
  29.8 0.0 copy-done
  29.8 0.0 copy-done.1
  29.8 0.0 copy-done.4
  29.8 1.7 %shard_map.85 = bf16[8,192,128]{2,1,0:T(8,128)(2,1)S(1)} custom-call(s32[2]{0:T(128)S(1)} %copy-done.4, bf16[2,128,768]{2,1,0:T(8,128)(2,1)S(1)} %bitcast.4, bf16[50,2,1536]{2,1,0:T(2,128)(2,1)S(1)} %copy-done.3, bf16[1536,384]{1,0:T(8,128)(2,1)S(1)} %copy-done, bf16[1536,384]{1,0:T(8,128)(2,1)S(1)} %copy-done.1, bf16[1536,384]{1,0:T(8,128)(2,1)S(1)} %copy-done.2), custom_call_target="tpu_custom_call" | custom-call | tf_op jit(solution)/shard_map/pallas_call | solution.py:247
  31.5 21.3 %all_to_all.15.held_ref = bf16[8,192,128]{2,1,0:T(8,128)(2,1)S(1)} all-to-all(bf16[8,192,128]{2,1,0:T(8,128)(2,1)S(1)} %shard_map.85), channel_id=1, replica_groups={{0,2,4,6,8,10,12,14},{16,18,20,22,24,26,28,30},{32,34,36,38,40,42,44,46..., dimensions={0} | all-to-all | bytes 786432 | tf_op jit(solution)/shard_map/all_to_all | solution.py:311
  52.7 1.0 %shard_map.86 = bf16[4,8,128,128]{3,2,1,0:T(8,128)(2,1)} custom-call(bf16[8,192,128]{2,1,0:T(8,128)(2,1)S(1)} %all_to_all.15.held_ref), custom_call_target="tpu_custom_call" | custom-call | tf_op jit(solution)/shard_map/pallas_call | solution.py:247
  53.8 4.3 %all-to-all-start.1 = ((bf16[4,8,128,128]{3,2,1,0:T(8,128)(2,1)}), bf16[4,8,128,128]{3,2,1,0:T(8,128)(2,1)S(1)}, u32[]{:S(2)}, u32[]{:S(2)}) async-start(bf16[4,8,128,128]{3,2,1,0:T(8,128)(2,1)} %shard_map.86), calls=%async_computation.1 | async-start | bytes 2097152 | tf_op jit(solution)/shard_map/all_to_all | solution.py:319
  58.1 1.9 %shard_map.87 = (f32[1024,128]{1,0:T(8,128)S(1)}, f32[1024,128]{1,0:T(8,128)S(1)}) custom-call(bf16[8,192,128]{2,1,0:T(8,128)(2,1)S(1)} %all_to_all.15.held_ref), custom_call_target="tpu_custom_call" | custom-call | tf_op jit(solution)/shard_map/pallas_call | solution.py:247
  60.0 14.2 %all-to-all-done.1.kv_ref = bf16[4,8,128,128]{3,2,1,0:T(8,128)(2,1)S(1)} async-done(((bf16[4,8,128,128]{3,2,1,0:T(8,128)(2,1)}), bf16[4,8,128,128]{3,2,1,0:T(8,128)(2,1)S(1)}, u32[]{:S(2)}, u32[]{:S(2)}) %all-to-all-start.1) | async-done | bytes 1048608 | tf_op jit(solution)/shard_map/all_to_all | solution.py:319
  74.2 3.9 %shard_map.88 = bf16[8,64,128]{2,1,0:T(8,128)(2,1)S(1)} custom-call(s32[1]{0:T(128)} %bitcast.x_ref, bf16[8,192,128]{2,1,0:T(8,128)(2,1)S(1)} %all_to_all.15.held_ref, bf16[4,8,128,128]{3,2,1,0:T(8,128)(2,1)S(1)} %all-to-all-done.1.kv_ref, f32[1024,128]{1,0:T(8,128)S(1)} %get-tuple-element.11.top_ref, f32[1024,128]{1,0:T(8,128)S(1)} %get-tuple-element.12.sum_ref), custom_call_target="tpu_custom_call" | custom-call | tf_op jit(solution)/shard_map/pallas_call | solution.py:247
  78.2 12.1 %all_to_all.16.in_ref = bf16[8,64,128]{2,1,0:T(8,128)(2,1)S(1)} all-to-all(bf16[8,64,128]{2,1,0:T(8,128)(2,1)S(1)} %shard_map.88), channel_id=1, replica_groups={{0,2,4,6,8,10,12,14},{16,18,20,22,24,26,28,30},{32,34,36,38,40,42,44,46..., dimensions={0} | all-to-all | bytes 262144 | tf_op jit(solution)/shard_map/all_to_all | solution.py:333
  90.3 0.7 shard_map.89
  (8 shorter events, 0.1 us)
Async XLA Ops:
  0.0 16.8 %copy-start.5 = (bf16[3,3,3,1536]{3,2,1,0:T(4,128)(2,1)S(1)}, bf16[3,3,3,1536]{3,2,1,0:T(4,128)(2,1)}, u32[]{:S(2)}) copy-start(bf16[3,3,3,1536]{3,2,1,0:T(4,128)(2,1)} %param.10) | copy-start | bytes 248836
  1.7 6.8 %collective-permute-start = (bf16[2,32,768]{2,1,0:T(8,128)(2,1)S(1)}, bf16[2,32,768]{2,1,0:T(8,128)(2,1)S(1)}, u32[]{:S(2)}, u32[]{:S(2)}) collective-permute-start(bf16[2,32,768]{2,1,0:T(8,128)(2,1)S(1)} %get-tuple-element.9.second_ref), channel_id=1, source_target_pairs={{0,64},{64,128},{128,192},{192,256},{256,320},{320,384},{384,448},... | collective-permute-start | bytes 294920 | tf_op jit(solution)/shard_map/ppermute | solution.py:104
  3.6 8.2 %collective-permute-start.1 = (bf16[2,32,768]{2,1,0:T(8,128)(2,1)S(1)}, bf16[2,32,768]{2,1,0:T(8,128)(2,1)S(1)}, u32[]{:S(2)}, u32[]{:S(2)}) collective-permute-start(bf16[2,32,768]{2,1,0:T(8,128)(2,1)S(1)} %get-tuple-element.10.first_ref), channel_id=1, source_target_pairs={{64,0},{128,64},{192,128},{256,192},{320,256},{384,320},{448,384},... | collective-permute-start | bytes 294920 | tf_op jit(solution)/shard_map/ppermute | solution.py:104
  11.8 18.0 %copy-start.3 = (bf16[50,2,1536]{2,1,0:T(2,128)(2,1)S(1)}, bf16[50,2,1536]{2,1,0:T(2,128)(2,1)}, u32[]{:S(2)}) copy-start(bf16[50,2,1536]{2,1,0:T(2,128)(2,1)} %modulation_ref.1) | copy-start | bytes 921604
  11.8 18.0 %copy-start.2 = (bf16[1536,384]{1,0:T(8,128)(2,1)S(1)}, bf16[1536,384]{1,0:T(8,128)(2,1)}, u32[]{:S(2)}) copy-start(bf16[1536,384]{1,0:T(8,128)(2,1)} %wv_ref.1) | copy-start | bytes 3538948
  11.9 6.8 %collective-permute-start.2 = (bf16[4,32,768]{2,1,0:T(8,128)(2,1)S(1)}, bf16[4,32,768]{2,1,0:T(8,128)(2,1)S(1)}, u32[]{:S(2)}, u32[]{:S(2)}) collective-permute-start(bf16[4,32,768]{2,1,0:T(8,128)(2,1)S(1)} %pad_maximum_fusion), channel_id=1, source_target_pairs={{0,2},{2,4},{4,6},{6,8},{8,10},{10,12},{12,14},{14,16},{16,18},{18... | collective-permute-start | bytes 589832 | tf_op jit(solution)/shard_map/ppermute | solution.py:104
  15.5 7.6 %collective-permute-start.3 = (bf16[4,32,768]{2,1,0:T(8,128)(2,1)S(1)}, bf16[4,32,768]{2,1,0:T(8,128)(2,1)S(1)}, u32[]{:S(2)}, u32[]{:S(2)}) collective-permute-start(bf16[4,32,768]{2,1,0:T(8,128)(2,1)S(1)} %pad_maximum_fusion.1), channel_id=1, source_target_pairs={{2,0},{4,2},{6,4},{8,6},{10,8},{12,10},{14,12},{16,14},{18,16},{20... | collective-permute-start | bytes 589832 | tf_op jit(solution)/shard_map/ppermute | solution.py:104
  16.9 12.9 %copy-start = (bf16[1536,384]{1,0:T(8,128)(2,1)S(1)}, bf16[1536,384]{1,0:T(8,128)(2,1)}, u32[]{:S(2)}) copy-start(bf16[1536,384]{1,0:T(8,128)(2,1)} %wq_ref.1) | copy-start | bytes 3538948
  16.9 12.9 %copy-start.1 = (bf16[1536,384]{1,0:T(8,128)(2,1)S(1)}, bf16[1536,384]{1,0:T(8,128)(2,1)}, u32[]{:S(2)}) copy-start(bf16[1536,384]{1,0:T(8,128)(2,1)} %wk_ref.1) | copy-start | bytes 3538948
  16.9 12.9 %copy-start.4 = (s32[2]{0:T(128)S(1)}, s32[2]{0:T(128)}, u32[]{:S(2)}) copy-start(s32[2]{0:T(128)} %step_ref.1) | copy-start | bytes 28
  53.8 20.4 %all-to-all-start.1 = ((bf16[4,8,128,128]{3,2,1,0:T(8,128)(2,1)}), bf16[4,8,128,128]{3,2,1,0:T(8,128)(2,1)S(1)}, u32[]{:S(2)}, u32[]{:S(2)}) async-start(bf16[4,8,128,128]{3,2,1,0:T(8,128)(2,1)} %shard_map.86), calls=%async_computation.1 | async-start | bytes 2097152 | tf_op jit(solution)/shard_map/all_to_all | solution.py:319

commit v5 on v4

--- a/solution.py
+++ b/solution.py
@@ -7,11 +7,41 @@
 
 HEAD_DIM = 64
 LANES = 128
-ROWS = 4
-COLS = 8
+ROWS, COLS = 4, 8
+BLOCKS = (2, 4)
+PLACES = (2, 2)
+SLOTS = 8
+COPIES = 4
+FRAMES = 8
+
+
 LOG2E = 1.4426950408889634
-X_GROUPS = [[x * COLS + y for x in range(ROWS)] for y in range(COLS)]
-Y_GROUPS = [[x * COLS + y for y in range(COLS)] for x in range(ROWS)]
+
+
+def device_at(frame, block, place):
+    x = 2 * block[0] + (place[0] + block[0]) % 2 + frame % 2
+    y = 2 * block[1] + place[1] + frame % 2
+    return (frame * ROWS + x % ROWS) * COLS + y % COLS
+
+
+def pairs(sizes):
+    return [(i, j) for i in range(sizes[0]) for j in range(sizes[1])]
+
+
+HEAD_GROUPS = [
+    [device_at(f, block, place) for block in pairs(BLOCKS)]
+    for f in range(FRAMES)
+    for place in pairs(PLACES)
+]
+KEY_GROUPS = [
+    [device_at(f, block, place) for place in pairs(PLACES)]
+    for f in range(FRAMES)
+    for block in pairs(BLOCKS)
+]
+
+
+def exchange(x, groups):
+    return lax.all_to_all(x, ("frame", "patch"), 0, 0, axis_index_groups=groups)
 
 
 BLOCK = 64
@@ -112,7 +142,14 @@
     return pltpu.roll(x, HEAD_DIM, x.ndim - 1)
 
 
-def project_kernel(step_ref, mixed_ref, modulation_ref, wq_ref, wk_ref, wv_ref, out_ref):
+def pick_kernel(step_ref, modulation_ref, shift_ref, scale_ref):
+    for f in range(shift_ref.shape[0]):
+        picked = modulation_ref[step_ref[f]].astype(jnp.float32)
+        shift_ref[f : f + 1, :] = picked[0:1]
+        scale_ref[f : f + 1, :] = picked[1:2]
+
+
+def project_kernel(mixed_ref, shift_ref, scale_ref, wq_ref, wk_ref, wv_ref, out_ref):
     half = mixed_ref.shape[1] // 2
     parts = []
     for f in range(2):
@@ -123,8 +160,7 @@
         centered = x - average
         variance = jnp.mean(centered * centered, axis=1, keepdims=True)
         x = centered * lax.rsqrt(variance + 1e-06)
-        picked = modulation_ref[step_ref[f]].astype(jnp.float32)
-        x = x * (1.0 + picked[1:2]) + picked[0:1]
+        x = x * (1.0 + scale_ref[f : f + 1, :]) + shift_ref[f : f + 1, :]
         parts.append(x.astype(jnp.bfloat16))
     normed = jnp.concatenate(parts, axis=0)
     tokens = 2 * half
@@ -170,58 +206,30 @@
 FACTOR = LOG2E * HEAD_DIM ** (-0.5)
 
 
-def copies_kernel(held_ref, out_ref, sems):
+def copies_kernel(held_ref, out_ref):
     tokens = out_ref.shape[2]
-    copies = [
-        pltpu.make_async_copy(held_ref.at[:, pl.ds(0, tokens), :], out_ref.at[x], sems.at[x])
-        for x in range(out_ref.shape[0])
-    ]
-    for copy in copies:
-        copy.start()
-    for copy in copies:
-        copy.wait()
-
-
-def attend_own_kernel(held_ref, top_ref, sum_ref):
-    slots, width, _ = held_ref.shape
-    tokens = width * 2 // 3
-    kv = held_ref[:, :tokens, :].reshape(slots * tokens, LANES)
+    kv = held_ref[:, :tokens, :]
+    for x in range(out_ref.shape[0]):
+        out_ref[x] = kv
+
+
+def attend_kernel(held_ref, kv_ref, out_ref):
+    slots, half, _ = out_ref.shape
+    kv = kv_ref[...].reshape(-1, LANES)
     values = counted(kv)
     step = slots // 2
-    rows = step * tokens
-    for start in range(0, slots, step):
-        scores = scored(query_rows(held_ref, start, step), kv)
-        top = jnp.max(scores, axis=1, keepdims=True)
-        weights = jnp.exp2((scores - top) * FACTOR).astype(jnp.bfloat16)
-        place = slice(start * tokens, start * tokens + rows)
-        top_ref[place, :] = jnp.broadcast_to(top, (rows, LANES))
-        sum_ref[place, :] = jnp.dot(weights, values, preferred_element_type=jnp.float32)
-
-
-def attend_kernel(x_ref, held_ref, kv_ref, top_ref, sum_ref, out_ref):
-    slots, width, _ = held_ref.shape
-    tokens = width * 2 // 3
-    half = tokens // 2
-    others = [lax.rem(x_ref[0] + j, ROWS) for j in range(1, ROWS)]
-    kv = jnp.concatenate([kv_ref[x].reshape(slots * tokens, LANES) for x in others], axis=0)
-    values = counted(kv)
-    step = slots // 2
-    rows = step * tokens
-    low = low_lanes((rows // 2, LANES))
+    low = low_lanes((step * half, LANES))
     starts = list(range(0, slots, step))
     scores = scored(query_rows(held_ref, 0, step), kv)
     for start in starts:
         later = None
         if start != starts[-1]:
             later = scored(query_rows(held_ref, start + step, step), kv)
-        place = slice(start * tokens, start * tokens + rows)
-        own_top = top_ref[place, :][:, :1]
-        top = jnp.maximum(jnp.max(scores, axis=1, keepdims=True), own_top)
+        top = jnp.max(scores, axis=1, keepdims=True)
         weights = jnp.exp2((scores - top) * FACTOR).astype(jnp.bfloat16)
         summed = jnp.dot(weights, values, preferred_element_type=jnp.float32)
-        summed = summed + sum_ref[place, :] * jnp.exp2((own_top - top) * FACTOR)
         done = summed / swap(summed)
-        result = jnp.where(low, swap(done[: rows // 2]), done[rows // 2 :])
+        result = jnp.where(low, swap(done[: step * half]), done[step * half :])
         out_ref[start : start + step] = result.astype(jnp.bfloat16).reshape(step, half, LANES)
         scores = later
 
@@ -242,13 +250,13 @@
 HBM = pl.BlockSpec(memory_space=pltpu.HBM)
 
 
-def call(kernel, shapes, *args, spaces=None, out_space=VMEM, scratch=()):
+def call(kernel, shapes, *args, spaces=None, scratch=()):
     shapes = [jax.ShapeDtypeStruct(shape, kind) for shape, kind in shapes]
     return pl.pallas_call(
         kernel,
         out_shape=shapes,
         in_specs=spaces or [VMEM] * len(args),
-        out_specs=[out_space] * len(shapes),
+        out_specs=[VMEM] * len(shapes),
         scratch_shapes=scratch,
         compiler_params=pltpu.CompilerParams(vmem_limit_bytes=48 * 1024 * 1024),
     )(*args)
@@ -272,6 +280,13 @@
     pair_index = lax.axis_index("tp")
     taps = lax.dynamic_slice_in_dim(conv_weight, pair_index * channels, channels, 3)
     taps = taps.reshape(27, channels).astype(wide)
+    shift, scale = call(
+        pick_kernel,
+        [((frames, modulation.shape[2]), wide)] * 2,
+        timestep,
+        modulation,
+        spaces=[SMEM, VMEM],
+    )
 
     frame_shape = ((tile_rows, tile_cols, channels), narrow)
     by_group = exponents.transpose(0, 3, 1, 2)
@@ -299,38 +314,19 @@
     mixed = lax.all_gather(mixed_half, "tp", axis=0)
     (send,) = call(
         project_kernel,
-        [((COLS, tokens + half, LANES), narrow)],
-        timestep,
+        [((SLOTS, tokens + half, LANES), narrow)],
         mixed,
-        modulation,
+        shift,
+        scale,
         query_weight,
         key_weight,
         value_weight,
-        spaces=[SMEM] + [VMEM] * 5,
-    )
-    held = lax.all_to_all(send, "patch", 0, 0, axis_index_groups=Y_GROUPS)
-    (copies,) = call(
-        copies_kernel,
-        [((ROWS, COLS, tokens, LANES), narrow)],
-        held,
-        out_space=HBM,
-        scratch=[pltpu.SemaphoreType.DMA((ROWS,))],
-    )
-    kv = lax.all_to_all(copies, "patch", 0, 0, axis_index_groups=X_GROUPS)
-    partial = ((COLS * tokens, LANES), wide)
-    top, summed = call(attend_own_kernel, [partial] * 2, held)
-    x_index = (lax.axis_index("patch") // COLS).reshape(1)
-    (result,) = call(
-        attend_kernel,
-        [((COLS, half, LANES), narrow)],
-        x_index,
-        held,
-        kv,
-        top,
-        summed,
-        spaces=[SMEM] + [VMEM] * 4,
-    )
-    back = lax.all_to_all(result, "patch", 0, 0, axis_index_groups=Y_GROUPS)
+    )
+    held = exchange(send, HEAD_GROUPS)
+    (copies,) = call(copies_kernel, [((COPIES, SLOTS, tokens, LANES), narrow)], held)
+    kv = exchange(copies, KEY_GROUPS)
+    (result,) = call(attend_kernel, [((SLOTS, half, LANES), narrow)], held, kv)
+    back = exchange(result, HEAD_GROUPS)
     (out,) = call(unpack_kernel, [((frames, half, local_width), narrow)], back)
     return out.reshape(frames, tile_rows, tile_cols, local_width)
 

time: 91.4 us -> 88 us (0.963)
  the two profiles are of different devices: /device:TPU:128 before, /device:TPU:256 now
where the time goes in v5:
time: 88 us; the launch traced here: 87.7 us
  blocking collectives  56.7 us (64%)
  starting transfers between devices  12.6 us (14%)
  Pallas kernels  9.9 us (11%)
  waiting for transfers between devices  8.16 us (9%)
    all_to_all x3, blocking collectives, exchange(): return lax.all_to_all(x, ('frame', 'patch'), 0, 0, axis_index_groups=groups)  48.2 us
    ppermute x4, starting transfers between devices, neighbours(): return (lax.ppermute(last, axis, up), lax.ppermute(first, axis, down))  12.6 us
    pallas_call x8, Pallas kernels, call(): pl.pallas_call(kernel, out_shape=shapes, in_specs=spaces or [VMEM] * len(...  9.9 us
    all_gather x1, blocking collectives, local(): mixed = lax.all_gather(mixed_half, 'tp', axis=0)  8.46 us
    ppermute x4, waiting for transfers between devices, neighbours(): return (lax.ppermute(last, axis, up), lax.ppermute(first, axis, down))  8.16 us
  transfers between devices with their start and end apart: 4, of which 4 were waited for; matrix products, arithmetic and copies ran while one was open for 0% of the time, Pallas kernels for 1%

profile of v5, /device:TPU:256, one launch (start us, length us, event | category | flops | bytes accessed | tf_op | source)
XLA Modules:
  0.0 87.7 jit_solution(2852851560042591305)
XLA Ops:
  0.0 0.0 copy-start.5
  0.0 0.0 copy-start.3
  0.0 0.0 copy-start.4
  0.0 1.7 %shard_map.82 = (bf16[2,32,768]{2,1,0:T(8,128)(2,1)S(1)}, bf16[2,32,768]{2,1,0:T(8,128)(2,1)S(1)}) custom-call(s32[2,2,32,768]{3,2,1,0:T(8,128)} %codes_ref.1, s32[2,12,2,32]{3,2,1,0:T(2,128)} %bitcast.4), custom_call_target="tpu_custom_call" | custom-call | tf_op jit(solution)/shard_map/pallas_call | solution.py:255
  1.7 1.9 %collective-permute-start = (bf16[2,32,768]{2,1,0:T(8,128)(2,1)S(1)}, bf16[2,32,768]{2,1,0:T(8,128)(2,1)S(1)}, u32[]{:S(2)}, u32[]{:S(2)}) collective-permute-start(bf16[2,32,768]{2,1,0:T(8,128)(2,1)S(1)} %get-tuple-element.9.second_ref), channel_id=1, source_target_pairs={{0,64},{64,128},{128,192},{192,256},{256,320},{320,384},{384,448},... | collective-permute-start | bytes 294920 | tf_op jit(solution)/shard_map/ppermute | solution.py:134
  3.6 5.8 %collective-permute-start.1 = (bf16[2,32,768]{2,1,0:T(8,128)(2,1)S(1)}, bf16[2,32,768]{2,1,0:T(8,128)(2,1)S(1)}, u32[]{:S(2)}, u32[]{:S(2)}) collective-permute-start(bf16[2,32,768]{2,1,0:T(8,128)(2,1)S(1)} %get-tuple-element.10.first_ref), channel_id=1, source_target_pairs={{64,0},{128,64},{192,128},{256,192},{320,256},{384,320},{448,384},... | collective-permute-start | bytes 294920 | tf_op jit(solution)/shard_map/ppermute | solution.py:134
  9.4 0.4 collective-permute-done.before_ref
  9.9 1.8 %collective-permute-done.1.after_ref = bf16[2,32,768]{2,1,0:T(8,128)(2,1)S(1)} collective-permute-done((bf16[2,32,768]{2,1,0:T(8,128)(2,1)S(1)}, bf16[2,32,768]{2,1,0:T(8,128)(2,1)S(1)}, u32[]{:S(2)}, u32[]{:S(2)}) %collective-permute-start.1) | collective-permute-done | bytes 98336 | tf_op jit(solution)/shard_map/ppermute | solution.py:134
  11.7 3.5 %collective-permute-start.2 = (bf16[4,32,768]{2,1,0:T(8,128)(2,1)S(1)}, bf16[4,32,768]{2,1,0:T(8,128)(2,1)S(1)}, u32[]{:S(2)}, u32[]{:S(2)}) collective-permute-start(bf16[4,32,768]{2,1,0:T(8,128)(2,1)S(1)} %pad_maximum_fusion), channel_id=1, source_target_pairs={{0,2},{2,4},{4,6},{6,8},{8,10},{10,12},{12,14},{14,16},{16,18},{18... | collective-permute-start | bytes 589832 | tf_op jit(solution)/shard_map/ppermute | solution.py:134
  15.2 0.0 copy-start.2
  15.2 1.4 %collective-permute-start.3 = (bf16[4,32,768]{2,1,0:T(8,128)(2,1)S(1)}, bf16[4,32,768]{2,1,0:T(8,128)(2,1)S(1)}, u32[]{:S(2)}, u32[]{:S(2)}) collective-permute-start(bf16[4,32,768]{2,1,0:T(8,128)(2,1)S(1)} %pad_maximum_fusion.1), channel_id=1, source_target_pairs={{2,0},{4,2},{6,4},{8,6},{10,8},{12,10},{14,12},{16,14},{18,16},{20... | collective-permute-start | bytes 589832 | tf_op jit(solution)/shard_map/ppermute | solution.py:134
  16.6 0.0 copy-done.5
  16.7 0.0 copy-done.3
  16.7 0.0 copy-done.4
  16.8 0.6 shard_map.85
  17.3 0.0 copy-start
  17.3 0.0 copy-start.1
  17.3 0.6 shard_map.83.part_ref
  17.9 1.1 %collective-permute-done.2.above_ref = bf16[4,32,768]{2,1,0:T(8,128)(2,1)S(1)} collective-permute-done((bf16[4,32,768]{2,1,0:T(8,128)(2,1)S(1)}, bf16[4,32,768]{2,1,0:T(8,128)(2,1)S(1)}, u32[]{:S(2)}, u32[]{:S(2)}) %collective-permute-start.2) | collective-permute-done | bytes 196640 | tf_op jit(solution)/shard_map/ppermute | solution.py:134
  19.0 4.9 %collective-permute-done.3.below_ref = bf16[4,32,768]{2,1,0:T(8,128)(2,1)S(1)} collective-permute-done((bf16[4,32,768]{2,1,0:T(8,128)(2,1)S(1)}, bf16[4,32,768]{2,1,0:T(8,128)(2,1)S(1)}, u32[]{:S(2)}, u32[]{:S(2)}) %collective-permute-start.3) | collective-permute-done | bytes 196640 | tf_op jit(solution)/shard_map/ppermute | solution.py:134
  23.9 0.3 shard_map.84
  24.2 8.5 %all-gather = bf16[256,768]{1,0:T(8,128)(2,1)S(1)} all-gather(bf16[128,768]{1,0:T(8,128)(2,1)S(1)} %shard_map.84), channel_id=2, replica_groups=mesh['frame'=8,'patch'=32,'tp'=2] {'tp'}, dimensions={0}, use_global_device_ids=true | all-gather | bytes 589824 | tf_op jit(solution)/shard_map/all_gather | solution.py:314
  32.7 0.0 copy-done.2
  32.7 0.0 copy-done
  32.7 0.0 copy-done.1
  32.7 1.1 %shard_map.86 = bf16[8,192,128]{2,1,0:T(8,128)(2,1)S(1)} custom-call(bf16[2,128,768]{2,1,0:T(8,128)(2,1)S(1)} %bitcast.3, f32[2,1536]{1,0:T(2,128)S(1)} %get-tuple-element.11.shift_ref, f32[2,1536]{1,0:T(2,128)S(1)} %get-tuple-element.12.scale_ref, bf16[1536,384]{1,0:T(8,128)(2,1)S(1)} %copy-done, bf16[1536,384]{1,0:T(8,128)(2,1)S(1)} %copy-done.1, ...), custom_call_target="tpu_custom_call" | custom-call | tf_op jit(solution)/shard_map/pallas_call | solution.py:255
  33.8 22.2 %all_to_all.15.held_ref = bf16[8,192,128]{2,1,0:T(8,128)(2,1)S(1)} all-to-all(bf16[8,192,128]{2,1,0:T(8,128)(2,1)S(1)} %shard_map.86), channel_id=1, replica_groups={{0,4,8,12,48,52,56,60},{2,6,10,14,50,54,58,62},{16,20,24,28,32,36,40,44..., dimensions={0} | all-to-all | bytes 786432 | tf_op jit(solution)/shard_map/all_to_all | solution.py:44
  56.0 0.1 shard_map.87
  56.1 12.4 %all_to_all.16.kv_ref = bf16[4,8,128,128]{3,2,1,0:T(8,128)(2,1)S(1)} all-to-all(bf16[4,8,128,128]{3,2,1,0:T(8,128)(2,1)S(1)} %shard_map.87), channel_id=1, replica_groups={{0,2,16,18},{4,6,20,22},{8,10,24,26},{12,14,28,30},{48,50,32,34},{52,54..., dimensions={0} | all-to-all | bytes 2097152 | tf_op jit(solution)/shard_map/all_to_all | solution.py:44
  68.5 4.8 %shard_map.88 = bf16[8,64,128]{2,1,0:T(8,128)(2,1)S(1)} custom-call(bf16[8,192,128]{2,1,0:T(8,128)(2,1)S(1)} %all_to_all.15.held_ref, bf16[4,8,128,128]{3,2,1,0:T(8,128)(2,1)S(1)} %all_to_all.16.kv_ref), custom_call_target="tpu_custom_call" | custom-call | tf_op jit(solution)/shard_map/pallas_call | solution.py:255
  73.3 13.6 %all_to_all.17.in_ref = bf16[8,64,128]{2,1,0:T(8,128)(2,1)S(1)} all-to-all(bf16[8,64,128]{2,1,0:T(8,128)(2,1)S(1)} %shard_map.88), channel_id=1, replica_groups={{0,4,8,12,48,52,56,60},{2,6,10,14,50,54,58,62},{16,20,24,28,32,36,40,44..., dimensions={0} | all-to-all | bytes 262144 | tf_op jit(solution)/shard_map/all_to_all | solution.py:44
  86.9 0.7 shard_map.89
  (7 shorter events, 0.1 us)
Async XLA Ops:
  0.0 16.6 %copy-start.5 = (bf16[3,3,3,1536]{3,2,1,0:T(4,128)(2,1)S(1)}, bf16[3,3,3,1536]{3,2,1,0:T(4,128)(2,1)}, u32[]{:S(2)}) copy-start(bf16[3,3,3,1536]{3,2,1,0:T(4,128)(2,1)} %param.10) | copy-start | bytes 248836
  0.0 16.7 %copy-start.3 = (bf16[50,2,1536]{2,1,0:T(2,128)(2,1)S(1)}, bf16[50,2,1536]{2,1,0:T(2,128)(2,1)}, u32[]{:S(2)}) copy-start(bf16[50,2,1536]{2,1,0:T(2,128)(2,1)} %modulation_ref.1) | copy-start | bytes 921604
  0.0 16.7 %copy-start.4 = (s32[2]{0:T(128)S(1)}, s32[2]{0:T(128)}, u32[]{:S(2)}) copy-start(s32[2]{0:T(128)} %step_ref.1) | copy-start | bytes 28
  1.7 8.1 %collective-permute-start = (bf16[2,32,768]{2,1,0:T(8,128)(2,1)S(1)}, bf16[2,32,768]{2,1,0:T(8,128)(2,1)S(1)}, u32[]{:S(2)}, u32[]{:S(2)}) collective-permute-start(bf16[2,32,768]{2,1,0:T(8,128)(2,1)S(1)} %get-tuple-element.9.second_ref), channel_id=1, source_target_pairs={{0,64},{64,128},{128,192},{192,256},{256,320},{320,384},{384,448},... | collective-permute-start | bytes 294920 | tf_op jit(solution)/shard_map/ppermute | solution.py:134
  3.6 8.0 %collective-permute-start.1 = (bf16[2,32,768]{2,1,0:T(8,128)(2,1)S(1)}, bf16[2,32,768]{2,1,0:T(8,128)(2,1)S(1)}, u32[]{:S(2)}, u32[]{:S(2)}) collective-permute-start(bf16[2,32,768]{2,1,0:T(8,128)(2,1)S(1)} %get-tuple-element.10.first_ref), channel_id=1, source_target_pairs={{64,0},{128,64},{192,128},{256,192},{320,256},{384,320},{448,384},... | collective-permute-start | bytes 294920 | tf_op jit(solution)/shard_map/ppermute | solution.py:134
  11.7 7.3 %collective-permute-start.2 = (bf16[4,32,768]{2,1,0:T(8,128)(2,1)S(1)}, bf16[4,32,768]{2,1,0:T(8,128)(2,1)S(1)}, u32[]{:S(2)}, u32[]{:S(2)}) collective-permute-start(bf16[4,32,768]{2,1,0:T(8,128)(2,1)S(1)} %pad_maximum_fusion), channel_id=1, source_target_pairs={{0,2},{2,4},{4,6},{6,8},{8,10},{10,12},{12,14},{14,16},{16,18},{18... | collective-permute-start | bytes 589832 | tf_op jit(solution)/shard_map/ppermute | solution.py:134
  15.2 17.5 %copy-start.2 = (bf16[1536,384]{1,0:T(8,128)(2,1)S(1)}, bf16[1536,384]{1,0:T(8,128)(2,1)}, u32[]{:S(2)}) copy-start(bf16[1536,384]{1,0:T(8,128)(2,1)} %wv_ref.1) | copy-start | bytes 3538948
  15.2 8.6 %collective-permute-start.3 = (bf16[4,32,768]{2,1,0:T(8,128)(2,1)S(1)}, bf16[4,32,768]{2,1,0:T(8,128)(2,1)S(1)}, u32[]{:S(2)}, u32[]{:S(2)}) collective-permute-start(bf16[4,32,768]{2,1,0:T(8,128)(2,1)S(1)} %pad_maximum_fusion.1), channel_id=1, source_target_pairs={{2,0},{4,2},{6,4},{8,6},{10,8},{12,10},{14,12},{16,14},{18,16},{20... | collective-permute-start | bytes 589832 | tf_op jit(solution)/shard_map/ppermute | solution.py:134
  17.3 15.3 %copy-start = (bf16[1536,384]{1,0:T(8,128)(2,1)S(1)}, bf16[1536,384]{1,0:T(8,128)(2,1)}, u32[]{:S(2)}) copy-start(bf16[1536,384]{1,0:T(8,128)(2,1)} %wq_ref.1) | copy-start | bytes 3538948
  17.3 15.3 %copy-start.1 = (bf16[1536,384]{1,0:T(8,128)(2,1)S(1)}, bf16[1536,384]{1,0:T(8,128)(2,1)}, u32[]{:S(2)}) copy-start(bf16[1536,384]{1,0:T(8,128)(2,1)} %wk_ref.1) | copy-start | bytes 3538948
